TPU v7x, 256 devices: a whole 4x4x8 slice. The times are simulated.
256 devices in a mesh: ctx: 32 (over z, y), mp: 8 (over x, core).
Axes of the slice: x: 4, y: 4, z: 8, core: 2. Of those that a mesh axis runs over, the one named last changes fastest.
Arguments:
- query_rows: bfloat16 [16384, 4096], P('ctx', 'mp'), may hold values from -6 to 6
- key_rows: bfloat16 [16384, 4096], P('ctx', 'mp'), may hold values from -6 to 6
- value_rows: bfloat16 [16384, 4096], P('ctx', 'mp'), may hold values from -6 to 6
- out_weight: bfloat16 [4096, 4096], P('mp'), may hold values from -0.375 to 0.375
- random_ids: int32 [128, 3], P('ctx'), may hold values from 0 to 127, as said below
- global_ids: int32 [2], replicated, may hold values from 0 to 127, as said below
Outputs:
- projected: bfloat16 [16384, 4096], P(('ctx', 'mp'))
Inputs may be any that keep to these rules, and one draw needn't show every extreme that they name: `random_ids`: take the 4 query blocks of one index of ctx and the aligned group of 4 key blocks of any one index of ctx: at most 2 of those query blocks' random ids (counted with repeats) fall in that group, and exactly 2 fall in some group in every draw. `global_ids`: two different block ids, one of them the document's last block.
All inputs are finite; a program needn't handle non-finite values.
Results may differ from a plain program's by a relative error of at most 0.02.
Values may be sent and summed in bfloat16 or wider, within the bound.
A program may use at most 128 MiB of HBM per device.

v0:
```python
import math

import jax
import jax.numpy as jnp
from jax import lax
from jax.sharding import PartitionSpec as P

HD = 128
BLK = 128
RAND = 3
GLOB = 2


def extended(cells, sides, width):
    for axis, dim in sides:
        count = lax.axis_size(axis)
        ends = count - 1
        head = lax.slice_in_dim(cells, 0, width, axis=dim)
        tail = lax.slice_in_dim(cells, cells.shape[dim] - width, cells.shape[dim], axis=dim)
        cells = jnp.concatenate(
            [
                lax.ppermute(tail, axis, [(i, (i + 1) % count) for i in range(ends)]),
                cells,
                lax.ppermute(head, axis, [((i + 1) % count, i) for i in range(ends)]),
            ],
            axis=dim,
        )
    return cells


def spread(array, axis, root):
    mine = lax.axis_index(axis) == root
    return lax.psum(jnp.where(mine, array, jnp.zeros_like(array)), axis)


def block_attend(query_block, pair_block):
    leading = query_block.shape[:-2]
    features = query_block.shape[-1]
    head_count = features // HD
    query_heads = query_block.reshape(leading + (BLK, head_count, HD))
    key_heads = pair_block[..., 0, :].reshape(leading + (BLK, head_count, HD))
    value_heads = pair_block[..., 1, :].reshape(leading + (BLK, head_count, HD))
    scores = jnp.einsum(
        "...qhd,...khd->...hqk", query_heads, key_heads, preferred_element_type=jnp.float32
    ) * (1.0 / math.sqrt(HD))
    maxima = jnp.max(scores, axis=-1)
    weights = jnp.exp(scores - maxima[..., None]).astype(jnp.bfloat16)
    totals = jnp.sum(weights, axis=-1, dtype=jnp.float32)
    outputs = jnp.einsum(
        "...hqk,...khd->...qhd", weights, value_heads, preferred_element_type=jnp.float32
    )
    return (outputs.reshape(leading + (BLK, features)), maxima, totals)


def shards(query_rows, key_rows, value_rows, out_weight, random_ids, global_ids):
    row_count, features = query_rows.shape
    per_device = row_count // BLK
    shard_count = lax.axis_size("ctx")
    position = lax.axis_index("ctx")
    total_blocks = per_device * shard_count
    head_count = features // HD
    query_blocks = query_rows.reshape(per_device, BLK, features)
    pair_rows = jnp.stack([key_rows, value_rows], axis=1)
    pair_blocks = pair_rows.reshape(per_device, BLK, 2, features)
    padded = extended(pair_rows, (("ctx", 0),), BLK)
    padded_blocks = padded.reshape(per_device + 2, BLK, 2, features)
    results = []
    usable = []
    first_blocks = position * per_device + jnp.arange(per_device, dtype=jnp.int32)
    for offset in range(3):
        results.append(block_attend(query_blocks, padded_blocks[offset : offset + per_device]))
        neighbour = first_blocks + offset - 1
        usable.append((neighbour >= 0) & (neighbour < total_blocks))
    owner_ids = global_ids // per_device
    local_index = global_ids % per_device
    tile_list = []
    for member in range(GLOB):
        own_piece = lax.dynamic_index_in_dim(pair_blocks, local_index[member], 0, keepdims=False)
        tile_list.append(spread(own_piece, "ctx", owner_ids[member]))
    global_tiles = jnp.stack(tile_list)
    for member in range(GLOB):
        shared = jnp.broadcast_to(global_tiles[member], (per_device,) + global_tiles.shape[1:])
        results.append(block_attend(query_blocks, shared))
        usable.append(jnp.ones((per_device,), jnp.bool_))
    requested = random_ids.reshape(-1)
    request_count = requested.shape[0]
    capacity = max(2, (request_count + shard_count - 1) // shard_count)
    slot_total = capacity * shard_count
    sources = requested // per_device
    wanted = requested % per_device
    positions = jnp.arange(request_count, dtype=jnp.int32)
    earlier = (sources[:, None] == sources[None, :]) & (positions[None, :] < positions[:, None])
    slot_index = sources * capacity + jnp.sum(earlier, axis=1)
    placed = jnp.arange(slot_total, dtype=jnp.int32)[:, None] == slot_index[None, :]
    send_ids = jnp.sum(jnp.where(placed, wanted[None, :], 0), axis=1).reshape(shard_count, capacity)
    asked_tiles = pair_blocks[
        lax.all_to_all(send_ids, "ctx", split_axis=0, concat_axis=0, tiled=True)
    ]
    fetched = lax.all_to_all(asked_tiles, "ctx", split_axis=0, concat_axis=0, tiled=True)
    chosen = fetched.reshape((slot_total,) + fetched.shape[2:])[slot_index]
    chosen = chosen.reshape((per_device, RAND) + chosen.shape[1:])
    for member in range(RAND):
        results.append(block_attend(query_blocks, chosen[:, member]))
    for member in range(RAND):
        usable.append(jnp.ones((per_device,), jnp.bool_))
    usable_all = jnp.stack(usable)[:, :, None, None]
    maxima_all = jnp.stack([result[1] for result in results])
    highest = jnp.max(jnp.where(usable_all, maxima_all, jnp.float32(-1e30)), axis=0)
    scales = jnp.where(usable_all, jnp.exp(maxima_all - highest[None]), jnp.float32(0.0))
    numerator = jnp.zeros((per_device, BLK, head_count, HD), jnp.float32)
    denominator = jnp.zeros((per_device, head_count, BLK), jnp.float32)
    for member, result in enumerate(results):
        numerator = (
            numerator
            + result[0].reshape(per_device, BLK, head_count, HD)
            * jnp.transpose(scales[member], (0, 2, 1))[..., None]
        )
        denominator = denominator + scales[member] * result[2]
    attended = (
        (numerator / jnp.transpose(denominator, (0, 2, 1))[..., None])
        .reshape(row_count, features)
        .astype(jnp.bfloat16)
    )
    projected = lax.psum_scatter(
        jnp.dot(attended, out_weight, preferred_element_type=jnp.float32).astype(jnp.bfloat16),
        "mp",
        scatter_dimension=0,
        tiled=True,
    )
    return projected


def solution(mesh):
    return jax.shard_map(
        shards,
        mesh=mesh,
        in_specs=(
            P("ctx", "mp"),
            P("ctx", "mp"),
            P("ctx", "mp"),
            P("mp", None),
            P("ctx", None),
            P(),
        ),
        out_specs=P(("ctx", "mp"), None),
        check_vma=False,
    )
```

profile of v0, /device:TPU:1, one launch (start us, length us, event | category | flops | bytes accessed | tf_op | source)
XLA Modules:
  0.0 577.5 jit_solution(15860030514979471795)
XLA Ops:
  8.3 12.0 %all-to-all-start = ((s32[32,1,2]{2,1,0:T(1,128)}), s32[32,1,2]{2,1,0:T(1,128)S(1)}, u32[]{:S(2)}, u32[]{:S(2)}) async-start(s32[32,1,2]{2,1,0:T(1,128)} %bitcast.25), calls=%async_computation | async-start | bytes 32768 | tf_op jit(solution)/shard_map/all_to_all | solution.py:97
  20.4 1.3 pad_maximum_fusion
  21.7 7.2 %all-to-all-done = s32[32,1,2]{2,1,0:T(1,128)S(1)} async-done(((s32[32,1,2]{2,1,0:T(1,128)}), s32[32,1,2]{2,1,0:T(1,128)S(1)}, u32[]{:S(2)}, u32[]{:S(2)}) %all-to-all-start) | async-done | bytes 288 | tf_op jit(solution)/shard_map/all_to_all | solution.py:97
  29.2 7.2 %gather_fusion = bf16[64,128,2,512]{3,1,2,0:T(8,128)(2,1)} fusion(bf16[4,128,2,512]{3,1,0,2:T(8,128)(2,1)S(1)} %pad_maximum_fusion, s32[1024]{0:T(1024)S(1)} %pad_clamp_fusion.1), kind=kCustom, calls=%fused_computation | custom fusion | bytes 33554688 | tf_op jit(solution)/shard_map/gather | solution.py:96
  36.4 5.3 all-to-all-start.1
  42.7 1.3 collective-permute-start.1
  44.0 4.7 collective-permute-start
  57.1 1.6 fusion.66
  59.3 1.3 convert_reduce_fusion.6
  60.6 45.4 %collective-permute-done.1 = bf16[128,2,512]{2,0,1:T(8,128)(2,1)S(1)} collective-permute-done((bf16[128,2,512]{2,0,1:T(8,128)(2,1)}, bf16[128,2,512]{2,0,1:T(8,128)(2,1)S(1)}, u32[]{:S(2)}, u32[]{:S(2)}) %collective-permute-start.1) | collective-permute-done | bytes 262176 | tf_op jit(solution)/shard_map/ppermute | solution.py:24
  105.9 2.1 pad_maximum_fusion.1
  108.0 1.1 fusion.60
  109.1 2.0 copy.155
  111.2 1.6 fusion.65
  112.8 1.2 fusion.59
  114.8 2.0 copy.154
  116.8 2.0 copy.162
  118.9 1.0 copy.183
  119.9 1.6 fusion.67
  121.5 337.9 %all-reduce.3.cloned.1.call-done = (bf16[128,2,512]{2,0,1:T(8,128)(2,1)}, bf16[128,2,512]{2,0,1:T(8,128)(2,1)}) async-done(((bf16[128,2,512]{2,0,1:T(8,128)(2,1)}, bf16[128,2,512]{2,0,1:T(8,128)(2,1)}), (bf16[128,2,512]{2,0,1:T(8,128)(2,1)}, bf16[128,2,512]{2,0,1:T(8,128)(2,1)})) %all-reduce.3.cloned.1.call-update) | async-done | bytes 524304 | tf_op jit(solution)/shard_map/psum | solution.py:33
  459.4 1.7 fusion.62
  461.8 1.6 fusion.61
  464.1 1.0 copy.210
  465.1 1.0 copy.211
  466.2 1.4 fusion.69
  467.6 1.0 copy-done.2
  469.3 1.4 fusion.68
  470.8 1.0 copy-done.4
  472.5 8.4 %gather_fusion.1 = bf16[12,128,2,512]{3,1,2,0:T(8,128)(2,1)} fusion(bf16[64,128,2,512]{3,1,2,0:T(8,128)(2,1)} %bitcast.28, s32[1024]{0:T(1024)} %pad_clamp_fusion), kind=kCustom, calls=%fused_computation.1 | custom fusion | bytes 6291504 | tf_op jit(solution)/shard_map/gather | solution.py:100
  480.9 3.5 slice_bitcast_fusion
  484.4 1.1 fusion.58
  485.4 2.0 copy.172
  487.5 2.5 fusion.70
  490.0 2.9 fusion.56
  493.0 2.1 copy.175
  495.0 2.5 fusion.71
  497.6 2.0 copy.178
  499.6 2.5 fusion.72
  504.3 2.1 copy.189
  506.3 2.0 copy.191
  508.4 2.1 copy.193
  510.4 1.4 convert_reduce_fusion
  511.9 1.4 convert_reduce_fusion.1
  513.3 1.5 fusion.21
  514.8 1.6 convert_reduce_fusion.2
  516.5 1.2 fusion.14
  521.7 6.5 %convolution_convert_fusion = bf16[512,4096]{1,0:T(8,128)(2,1)} fusion(bf16[512,4096]{1,0:T(8,128)(2,1)} %param.9, bf16[64,8,4,128]{3,2,1,0:T(4,128)(2,1)S(1)} %bitcast.242), kind=kOutput, calls=%fused_computation.2 | convolution fusion | flops 2149580800 | bytes 8912896 | tf_op jit(solution)/shard_map/dot_general | solution.py:125
  528.3 42.4 %reduce-scatter.2.cloned.1.call-done = bf16[64,4096]{1,0:T(8,128)(2,1)} async-done(((bf16[512,4096]{1,0:T(8,128)(2,1)}), bf16[64,4096]{1,0:T(8,128)(2,1)}) %reduce-scatter.2.cloned.1.call-update) | async-done | bytes 524304 | tf_op jit(solution)/shard_map/reduce_scatter | solution.py:124
  (142 shorter events, 17.0 us)
Async XLA Ops:
  8.3 20.5 %all-to-all-start = ((s32[32,1,2]{2,1,0:T(1,128)}), s32[32,1,2]{2,1,0:T(1,128)S(1)}, u32[]{:S(2)}, u32[]{:S(2)}) async-start(s32[32,1,2]{2,1,0:T(1,128)} %bitcast.25), calls=%async_computation | async-start | bytes 32768 | tf_op jit(solution)/shard_map/all_to_all | solution.py:97
  36.4 5.4 copy-start
  36.4 5.4 copy-start.1
  36.4 12.3 %copy-start.42 = (s32[2]{0:T(128)S(1)}, s32[2]{0:T(128)}, u32[]{:S(2)}) copy-start(s32[2]{0:T(128)} %param.11) | copy-start | bytes 28
  36.4 436.1 %all-to-all-start.1 = ((bf16[32,2,128,2,512]{4,2,3,1,0:T(8,128)(2,1)}), bf16[32,2,128,2,512]{4,2,3,1,0:T(8,128)(2,1)}, u32[]{:S(2)}, u32[]{:S(2)}) async-start(bf16[32,2,128,2,512]{4,2,3,1,0:T(8,128)(2,1)} %bitcast.218), calls=%async_computation.1 | async-start | bytes 33554432 | tf_op jit(solution)/shard_map/all_to_all | solution.py:99
  41.7 14.3 %copy-start.41 = (s32[4,3]{1,0:T(4,128)S(1)}, s32[4,3]{1,0:T(4,128)}, u32[]{:S(2)}) copy-start(s32[4,3]{1,0:T(4,128)} %param.10) | copy-start | bytes 148
  41.7 14.5 %copy-start.16 = (bf16[512,512]{1,0:T(8,128)(2,1)S(1)}, bf16[512,512]{1,0:T(8,128)(2,1)}, u32[]{:S(2)}) copy-start(bf16[512,512]{1,0:T(8,128)(2,1)} %param.6) | copy-start | bytes 1572868
  41.8 417.7 %all-reduce.3.cloned.1.call-start = ((), (), s32[]{:S(2)}) async-start(), calls=%async_computation.4 | async-start | bytes 1048576 | tf_op jit(solution)/shard_map/psum | solution.py:33
  42.7 63.3 %collective-permute-start.1 = (bf16[128,2,512]{2,0,1:T(8,128)(2,1)}, bf16[128,2,512]{2,0,1:T(8,128)(2,1)S(1)}, u32[]{:S(2)}, u32[]{:S(2)}) collective-permute-start(bf16[128,2,512]{2,0,1:T(8,128)(2,1)} %get-tuple-element.22), channel_id=1, source_target_pairs={{8,0},{16,8},{24,16},{32,24},{40,32},{48,40},{56,48},{64,56},{72,6... | collective-permute-start | bytes 786440 | tf_op jit(solution)/shard_map/ppermute | solution.py:24
  44.0 62.0 %collective-permute-start = (bf16[128,2,512]{2,0,1:T(8,128)(2,1)}, bf16[128,2,512]{2,0,1:T(8,128)(2,1)}, u32[]{:S(2)}, u32[]{:S(2)}) collective-permute-start(bf16[128,2,512]{2,0,1:T(8,128)(2,1)} %get-tuple-element.23), channel_id=1, source_target_pairs={{0,8},{8,16},{16,24},{24,32},{32,40},{40,48},{48,56},{56,64},{64,7... | collective-permute-start | bytes 786440 | tf_op jit(solution)/shard_map/ppermute | solution.py:22
  54.9 515.8 %reduce-scatter.2.cloned.1.call-start = ((), (), s32[]{:S(2)}) async-start(), calls=%async_computation.3 | async-start | bytes 4718592 | tf_op jit(solution)/shard_map/reduce_scatter | solution.py:124
  108.0 4.7 copy-start.9
  112.7 1.3 copy-start.8
  114.0 4.9 copy-start.15
  121.5 339.6 %copy-start.18 = (f32[4,4,128]{2,1,0:T(4,128)}, f32[4,4,128]{2,1,0:T(4,128)S(1)}, u32[]{:S(2)}) copy-start(f32[4,4,128]{2,1,0:T(4,128)S(1)} %get-tuple-element.50) | copy-start | bytes 24580
  467.6 1.0 copy-start.2
  467.6 13.3 %copy-start.20 = (f32[4,4,128]{2,1,0:T(4,128)}, f32[4,4,128]{2,1,0:T(4,128)S(1)}, u32[]{:S(2)}) copy-start(f32[4,4,128]{2,1,0:T(4,128)S(1)} %get-tuple-element.54) | copy-start | bytes 24580
  470.7 1.0 copy-start.4
  470.7 10.1 %copy-start.22 = (f32[4,4,128]{2,1,0:T(4,128)}, f32[4,4,128]{2,1,0:T(4,128)S(1)}, u32[]{:S(2)}) copy-start(f32[4,4,128]{2,1,0:T(4,128)S(1)} %get-tuple-element.52) | copy-start | bytes 24580
  490.0 12.1 %copy-start.24 = (f32[4,4,128]{2,1,0:T(4,128)}, f32[4,4,128]{2,1,0:T(4,128)S(1)}, u32[]{:S(2)}) copy-start(f32[4,4,128]{2,1,0:T(4,128)S(1)} %get-tuple-element.56) | copy-start | bytes 24580
  493.0 9.8 %copy-start.39 = (pred[8,4]{1,0:T(8,128)(4,1)S(1)}, pred[8,4]{1,0:T(8,128)(4,1)}, u32[]{:S(2)}) copy-start(pred[8,4]{1,0:T(8,128)(4,1)} %stack.51) | copy-start | bytes 100
  497.6 4.6 copy-start.26
  502.1 11.1 %copy-start.12 = (bf16[4,128,1,512]{1,3,0,2:T(8,128)(2,1)S(1)}, bf16[4,128,1,512]{1,3,0,2:T(8,128)(2,1)}, u32[]{:S(2)}) copy-start(bf16[4,128,1,512]{1,3,0,2:T(8,128)(2,1)} %copy.154) | copy-start | bytes 1572868
  503.6 6.8 %copy-start.29 = (f32[4,4,128]{2,1,0:T(4,128)S(1)}, f32[4,4,128]{2,1,0:T(4,128)}, u32[]{:S(2)}) copy-start(f32[4,4,128]{2,1,0:T(4,128)} %copy-done.28) | copy-start | bytes 24580
  503.6 8.2 %copy-start.27 = (f32[4,4,128]{2,1,0:T(4,128)S(1)}, f32[4,4,128]{2,1,0:T(4,128)}, u32[]{:S(2)}) copy-start(f32[4,4,128]{2,1,0:T(4,128)} %copy-done.26) | copy-start | bytes 24580
  508.4 6.4 %copy-start.19 = (f32[4,4,128]{2,1,0:T(4,128)S(1)}, f32[4,4,128]{2,1,0:T(4,128)}, u32[]{:S(2)}) copy-start(f32[4,4,128]{2,1,0:T(4,128)} %copy-done.18) | copy-start | bytes 24580
  508.4 6.5 %copy-start.25 = (f32[4,4,128]{2,1,0:T(4,128)S(1)}, f32[4,4,128]{2,1,0:T(4,128)}, u32[]{:S(2)}) copy-start(f32[4,4,128]{2,1,0:T(4,128)} %copy-done.24) | copy-start | bytes 24580
  511.8 4.6 copy-start.38
  514.8 2.9 copy-start.11
  514.8 2.9 copy-start.37
  516.5 1.6 copy-start.5
  516.5 1.6 copy-start.23
  516.5 1.6 copy-start.36
  517.7 1.2 copy-start.3
  517.7 1.2 copy-start.21
  517.7 1.2 copy-start.35
  518.1 1.3 copy-start.6
  518.1 1.4 copy-start.14
  518.1 1.4 copy-start.34
  518.9 1.3 copy-start.7
  518.9 1.5 copy-start.13
  519.5 1.2 copy-start.30
  519.5 1.2 copy-start.31
  519.5 1.2 copy-start.32
  519.5 1.2 copy-start.33
  519.5 1.4 copy-start.10
  519.5 1.5 copy-start.17
  519.6 1.5 copy-start.40
  (1 other events, 0.6 us)
Sparse Core Ops, SparseCore 0:
  55.0 404.3 all-reduce.2
  528.4 42.2 reduce-scatter.1
where the time goes:
time: 581 us; the launch traced here: 578 us
  waiting for transfers between devices  433 us (75%)
  local copies, waits for them, and re-layouts  61 us (10%)
  matrix products  26.3 us (5%)
  starting transfers between devices  23.6 us (4%)
  between operations  18.7 us (3%)
  other arithmetic  15 us (3%)
    psum x1, waiting for transfers between devices, spread(): return lax.psum(jnp.where(mine, array, jnp.zeros_like(array)), axis)  338 us
    ppermute x1, waiting for transfers between devices, extended(): lax.ppermute(head, axis, [((i + 1) % count, i) for i in range(ends)])  45.4 us
    reduce_scatter x1, waiting for transfers between devices, shards(): lax.psum_scatter(jnp.dot(attended, out_weight, preferred_element_type=jnp...  42.4 us
    slice x10, local copies, waits for them, and re-layouts, block_attend(): value_heads = pair_block[..., 1, :].reshape(leading + (BLK, head_count, HD))  17.8 us
    dot_general x8, matrix products, block_attend(): jnp.einsum('...qhd,...khd->...hqk', query_heads, key_heads, preferred_ele...  15.2 us
    all_to_all x1, starting transfers between devices, shards(): lax.all_to_all(send_ids, 'ctx', split_axis=0, concat_axis=0, tiled=True)  12 us
  transfers between devices with their start and end apart: 6, of which 4 were waited for; matrix products, arithmetic and copies ran while one was open for 6% of the time, Pallas kernels for 0%

commit v1 on v0

v1 whole, which is shorter than its diff:
```python
import math

import jax
import jax.numpy as jnp
from jax import lax
from jax.experimental import pallas as pl
from jax.experimental.pallas import tpu as pltpu
from jax.sharding import PartitionSpec as P

HD = 128
BLK = 128
RAND = 3
GLOB = 2
NZ = 8
NY = 4
NX = 4
HEADS = 4
QB = 4
ROWS = QB * BLK
FEATS = HEADS * HD
WIDTH = 4096
HALF = BLK // 2
SCALE = 1.0 / math.sqrt(HD)
LOW = -1e30
MESH = pl.DeviceIdType.MESH
NT = (((1,), (1,)), ((), ()))
TN = (((0,), (0,)), ((), ()))
RING = 14
MIB = 1024 * 1024


def any_spec():
    return pl.BlockSpec(memory_space=pl.ANY)


def vmem_spec():
    return pl.BlockSpec(memory_space=pltpu.VMEM)


def smem_spec():
    return pl.BlockSpec(memory_space=pltpu.SMEM)


def places():
    me = lax.axis_index("ctx")
    mp = lax.axis_index("mp")
    return me, me // NY, me % NY, mp, mp // 2, mp % 2


def gather_kernel(
    q_ref, k_ref, v_ref, w_ref, ids_ref,
    kcol, vcol, qrow, idrow, wsib, acc_out, stat_out,
    q_own, k_ext, v_ext,
    ring_send, ring_recv, row_send, row_recv, edge_send, edge_recv, w_sem, local_sem,
):
    me, z, y, mp, x, core = places()
    count = NZ * NY
    after, before = (me + 1) % count, (me + count - 1) % count
    sibling = mp + 1 - 2 * core
    up, down = (z + 1) % NZ, (z + NZ - 1) % NZ

    barrier = pltpu.get_barrier_semaphore()
    peers = [{"ctx": up * NY + y}, {"ctx": down * NY + y}]
    peers += [{"ctx": z * NY + (y + d) % NY} for d in range(1, NY)]
    peers += [{"ctx": after}, {"ctx": before}, {"mp": sibling}]
    for peer in peers:
        pl.semaphore_signal(barrier, inc=1, device_id=peer, device_id_type=MESH)
    pl.semaphore_wait(barrier, len(peers))

    def remote(src, dst, send, recv, peer):
        return pltpu.make_async_remote_copy(
            src_ref=src, dst_ref=dst, send_sem=send, recv_sem=recv, device_id=peer, device_id_type=MESH
        )

    edges = []
    for n, (own, ext) in enumerate(((k_ref, k_ext), (v_ref, v_ext))):
        edges.append(remote(own.at[pl.ds(ROWS - BLK, BLK)], ext.at[pl.ds(0, BLK)],
                            edge_send.at[2 * n], edge_recv.at[2 * n], {"ctx": after}))
        edges.append(remote(own.at[pl.ds(0, BLK)], ext.at[pl.ds(ROWS + BLK, BLK)],
                            edge_send.at[2 * n + 1], edge_recv.at[2 * n + 1], {"ctx": before}))

    def ring(way, i):
        sign = 1 if way == 0 else -1
        back, piece = i // 4, i % 4
        source = (z + NZ - sign * back) % NZ
        is_key = (piece < 2) == (way == 0)
        own, col = (k_ref, kcol) if is_key else (v_ref, vcol)
        rows = pl.ds((piece % 2) * (ROWS // 2), ROWS // 2)
        src = own.at[rows] if back == 0 else col.at[source, rows]
        peer = {"ctx": (up if way == 0 else down) * NY + y}
        return remote(src, col.at[source, rows], ring_send.at[way, i], ring_recv.at[way, i], peer)

    rings = [[ring(way, i) for i in range(RING)] for way in range(2)]
    rows = []
    for d in range(1, NY):
        peer = {"ctx": z * NY + (y + d) % NY}
        rows.append(remote(ids_ref, idrow.at[y], row_send.at[1, d - 1], row_recv.at[1, d - 1], peer))
        rows.append(remote(q_ref, qrow.at[y], row_send.at[0, d - 1], row_recv.at[0, d - 1], peer))
    weight = remote(w_ref, wsib, w_sem.at[0], w_sem.at[1], {"mp": sibling})

    for copy in edges:
        copy.start()
    for i in range(4):
        rings[0][i].start()
        rings[1][i].start()
    local = [
        pltpu.make_async_copy(q_ref, q_own, local_sem.at[0]),
        pltpu.make_async_copy(k_ref, k_ext.at[pl.ds(BLK, ROWS)], local_sem.at[1]),
        pltpu.make_async_copy(v_ref, v_ext.at[pl.ds(BLK, ROWS)], local_sem.at[2]),
        pltpu.make_async_copy(k_ref, kcol.at[z], local_sem.at[3]),
        pltpu.make_async_copy(v_ref, vcol.at[z], local_sem.at[4]),
        pltpu.make_async_copy(q_ref, qrow.at[y], local_sem.at[5]),
        pltpu.make_async_copy(ids_ref, idrow.at[y], local_sem.at[6]),
    ]
    for copy in local:
        copy.start()
    for copy in rows:
        copy.start()
    weight.start()
    for copy in local[:3]:
        copy.wait()
    for copy in edges:
        copy.wait_recv()

    def window(qb):
        row = lax.broadcasted_iota(jnp.int32, (3 * BLK, 1), 0)
        first = jnp.where(me + qb == 0, BLK, 0)
        last = jnp.where(me * QB + qb == count * QB - 1, 2 * BLK, 3 * BLK)
        live = (row >= first) & (row < last)
        span = pl.ds(pl.multiple_of(qb * BLK, BLK), 3 * BLK)
        for h in range(HEADS):
            cols = pl.ds(h * HD, HD)
            q = q_own[pl.ds(pl.multiple_of(qb * BLK, BLK), BLK), cols]
            s = lax.dot_general(k_ext[span, cols], q, NT, preferred_element_type=jnp.float32) * SCALE
            s = jnp.where(live, s, LOW)
            top = jnp.max(s, axis=0, keepdims=True)
            p = jnp.where(live, jnp.exp(s - top), 0.0).astype(jnp.bfloat16)
            stat_out[qb, pl.ds(h, 1), :] = top
            stat_out[qb, pl.ds(HEADS + h, 1), :] = jnp.sum(p.astype(jnp.float32), axis=0, keepdims=True)
            acc_out[qb, cols, :] = lax.dot_general(v_ext[span, cols], p, TN, preferred_element_type=jnp.float32)

    for i in range(RING):
        if i < QB:
            window(i)
        for way in range(2):
            rings[way][i].wait_recv()
            if i + 4 < RING:
                rings[way][i + 4].start()
    for copy in local[3:]:
        copy.wait()
    for copy in edges:
        copy.wait_send()
    for way in range(2):
        for i in range(RING):
            rings[way][i].wait_send()
    for copy in rows:
        copy.wait()
    weight.wait()


def gather(q, k, v, w, ids):
    bf, f32 = jnp.bfloat16, jnp.float32
    dma = pltpu.SemaphoreType.DMA
    return pl.pallas_call(
        gather_kernel,
        name="gather_and_window",
        out_shape=(
            jax.ShapeDtypeStruct((NZ, ROWS, FEATS), bf),
            jax.ShapeDtypeStruct((NZ, ROWS, FEATS), bf),
            jax.ShapeDtypeStruct((NY, ROWS, FEATS), bf),
            jax.ShapeDtypeStruct((NY, 8, 128), jnp.int32),
            jax.ShapeDtypeStruct((FEATS, WIDTH), bf),
            jax.ShapeDtypeStruct((QB, FEATS, BLK), f32),
            jax.ShapeDtypeStruct((QB, 2 * HEADS, BLK), f32),
        ),
        in_specs=[any_spec()] * 5,
        out_specs=(any_spec(),) * 5 + (vmem_spec(), vmem_spec()),
        scratch_shapes=[
            pltpu.VMEM((ROWS, FEATS), bf),
            pltpu.VMEM((ROWS + 2 * BLK, FEATS), bf),
            pltpu.VMEM((ROWS + 2 * BLK, FEATS), bf),
            dma((2, RING)), dma((2, RING)), dma((2, NY - 1)), dma((2, NY - 1)),
            dma((4,)), dma((4,)), dma((2,)), dma((7,)),
        ],
        compiler_params=pltpu.CompilerParams(
            collective_id=0, has_side_effects=True, vmem_limit_bytes=24 * MIB
        ),
        cost_estimate=pl.CostEstimate(flops=400 * 10**6, bytes_accessed=24 * MIB, transcendentals=0),
    )(q, k, v, w, ids)


def far_kernel(ids_ref, glob_ref, kcol, vcol, qrow, part_out, stat_out, acc, top_ref, sum_ref):
    y = lax.axis_index("ctx") % NY

    def attend(t, block):
        zs = lax.div(block, NY * QB)
        rows = pl.ds(pl.multiple_of(lax.rem(block, QB) * BLK, BLK), BLK)
        q_rows = pl.ds(pl.multiple_of(lax.rem(t, QB) * BLK, BLK), BLK)
        for h in range(HEADS):
            cols = pl.ds(h * HD, HD)
            q = qrow[lax.div(t, QB), q_rows, cols]
            s = lax.dot_general(kcol[zs, rows, cols], q, NT, preferred_element_type=jnp.float32) * SCALE
            old = top_ref[pl.ds(h, 1), :]
            top = jnp.maximum(old, jnp.max(s, axis=0, keepdims=True))
            p = jnp.exp(s - top).astype(jnp.bfloat16)
            fade = jnp.exp(old - top)
            top_ref[pl.ds(h, 1), :] = top
            sum_ref[pl.ds(h, 1), :] = sum_ref[pl.ds(h, 1), :] * fade + jnp.sum(
                p.astype(jnp.float32), axis=0, keepdims=True)
            acc[cols, :] = acc[cols, :] * fade + lax.dot_general(
                vcol[zs, rows, cols], p, TN, preferred_element_type=jnp.float32)

    def one(t, carry):
        acc[...] = jnp.zeros_like(acc)
        top_ref[...] = jnp.full_like(top_ref, LOW)
        sum_ref[...] = jnp.zeros_like(sum_ref)
        yd, qb = lax.div(t, QB), lax.rem(t, QB)
        for j in range(GLOB + RAND):
            block = glob_ref[j] if j < GLOB else ids_ref[yd, qb, j - GLOB]

            @pl.when(lax.rem(lax.div(block, QB), NY) == y)
            def _():
                attend(t, block)

        for h in range(HEADS):
            cols = pl.ds(h * HD, HD)
            total = sum_ref[pl.ds(h, 1), :]
            part_out[yd, qb, cols, :] = jnp.where(
                total > 0, acc[cols, :] / jnp.where(total > 0, total, 1.0), 0.0).astype(jnp.bfloat16)
            stat_out[yd, qb, pl.ds(h, 1), :] = top_ref[pl.ds(h, 1), :]
            stat_out[yd, qb, pl.ds(HEADS + h, 1), :] = total
        return carry

    lax.fori_loop(0, NY * QB, one, 0)


def far(idrow, globs, kcol, vcol, qrow):
    f32 = jnp.float32
    return pl.pallas_call(
        far_kernel,
        name="random_and_global",
        out_shape=(
            jax.ShapeDtypeStruct((NY, QB, FEATS, BLK), jnp.bfloat16),
            jax.ShapeDtypeStruct((NY, QB, 2 * HEADS, BLK), f32),
        ),
        in_specs=[smem_spec(), smem_spec(), vmem_spec(), vmem_spec(), vmem_spec()],
        out_specs=(vmem_spec(), vmem_spec()),
        scratch_shapes=[
            pltpu.VMEM((FEATS, BLK), f32), pltpu.VMEM((8, BLK), f32), pltpu.VMEM((8, BLK), f32),
        ],
        compiler_params=pltpu.CompilerParams(vmem_limit_bytes=40 * MIB),
        cost_estimate=pl.CostEstimate(flops=800 * 10**6, bytes_accessed=14 * MIB, transcendentals=0),
    )(idrow, globs, kcol, vcol, qrow)


def merge_kernel(
    acc_ref, wstat_ref, part, pstat, w_ref, wsib_ref, out_ref,
    got, got_stat, w_own, w_other, att, att_other, sent, relay, final, total,
    part_send, part_recv, stat_send, stat_recv, att_send, att_recv, x_send, x_recv, local_sem,
):
    me, z, y, mp, x, core = places()
    sibling = mp + 1 - 2 * core
    right, left = ((x + 1) % NX) * 2 + core, ((x + NX - 1) % NX) * 2 + core
    order = [(x + d) % NX for d in (2, 1, 3, 0)]

    barrier = pltpu.get_barrier_semaphore()
    peers = [{"ctx": z * NY + (y + d) % NY} for d in range(1, NY)]
    peers += [{"mp": sibling}, {"mp": right}, {"mp": left}]
    for peer in peers:
        pl.semaphore_signal(barrier, inc=1, device_id=peer, device_id_type=MESH)

    local = [
        pltpu.make_async_copy(part.at[y], got.at[NY - 1], local_sem.at[0]),
        pltpu.make_async_copy(pstat.at[y], got_stat.at[NY - 1], local_sem.at[1]),
        pltpu.make_async_copy(w_ref, w_own, local_sem.at[2]),
        pltpu.make_async_copy(wsib_ref, w_other, local_sem.at[3]),
    ]
    for copy in local:
        copy.start()
    pl.semaphore_wait(barrier, len(peers))

    def remote(src, dst, send, recv, peer):
        return pltpu.make_async_remote_copy(
            src_ref=src, dst_ref=dst, send_sem=send, recv_sem=recv, device_id=peer, device_id_type=MESH
        )

    stats, parts = [], []
    for d in range(1, NY):
        to = (y + d) % NY
        stats.append(remote(pstat.at[to], got_stat.at[d - 1], stat_send.at[d - 1], stat_recv.at[d - 1],
                            {"ctx": z * NY + to}))
        stats[-1].start()
    for i, qb in enumerate(order):
        parts.append([])
        for d in (2, 1, 3):
            to = (y + d) % NY
            parts[-1].append(remote(part.at[to, qb], got.at[d - 1, qb], part_send.at[d - 1, i],
                                    part_recv.at[d - 1, i], {"ctx": z * NY + to}))
            parts[-1][-1].start()
    for copy in stats:
        copy.wait_recv()
    for copy in local:
        copy.wait()

    swaps, sends = [], []
    mine = pl.ds(pl.multiple_of(core * HALF, HALF), HALF)
    theirs = pl.ds(pl.multiple_of((1 - core) * HALF, HALF), HALF)
    tile = 512
    middle = WIDTH // 2
    for i, qb in enumerate(order):
        for copy in parts[i]:
            copy.wait_recv()
        for h in range(HEADS):
            cols = pl.ds(h * HD, HD)
            tops = [wstat_ref[qb, pl.ds(h, 1), :]] + [got_stat[s, qb, pl.ds(h, 1), :] for s in range(NY)]
            sums = [wstat_ref[qb, pl.ds(HEADS + h, 1), :]] + [
                got_stat[s, qb, pl.ds(HEADS + h, 1), :] for s in range(NY)]
            best = tops[0]
            for top in tops[1:]:
                best = jnp.maximum(best, top)
            scales = [jnp.exp(top - best) for top in tops]
            weights = [scale * part_sum for scale, part_sum in zip(scales, sums)]
            low = weights[0] + weights[1] + weights[2] + weights[3] + weights[4]
            value = acc_ref[qb, cols, :] * (scales[0] / low)
            for s in range(NY):
                value += got[s, qb, cols, :].astype(jnp.float32) * (weights[s + 1] / low)
            att[i, :, cols] = value.T.astype(jnp.bfloat16)
        swaps.append(remote(att.at[i, theirs], att_other.at[i], att_send.at[i], att_recv.at[i], {"mp": sibling}))
        swaps[i].start()
        swaps[i].wait_recv()
        if i == 1:
            sends[0].wait_recv()
        if i == 2:
            sends[1].wait_recv()
        if i == 3:
            sends[2].wait_recv()
            sends[3].wait_recv()

        def project(n, carry):
            cols = pl.ds(pl.multiple_of(n * tile, tile), tile)
            value = jnp.dot(att[i, mine, :], w_own[:, cols], preferred_element_type=jnp.float32)
            value += jnp.dot(att_other[i], w_other[:, cols], preferred_element_type=jnp.float32)
            if i == 3:
                value += final[0, :, cols].astype(jnp.float32) + final[1, :, cols].astype(jnp.float32)
                out_ref[:, cols] = value.astype(jnp.bfloat16)
            else:
                total[:, cols] = value
            return carry

        lax.fori_loop(0, WIDTH // tile, project, 0)
        if i == 1:
            total[:, pl.ds(0, middle)] += relay[0].astype(jnp.float32)
        if i == 2:
            total[:, pl.ds(middle, middle)] += relay[1].astype(jnp.float32)
        if i < 3:
            sent[i] = total[...].astype(jnp.bfloat16)
        if i == 0:
            for s, peer in enumerate((right, left)):
                sends.append(remote(sent.at[0, :, pl.ds(s * middle, middle)], relay.at[s],
                                    x_send.at[s], x_recv.at[s], {"mp": peer}))
                sends[-1].start()
        elif i < 3:
            sends.append(remote(sent.at[i], final.at[i - 1], x_send.at[i + 1], x_recv.at[i + 1],
                                {"mp": right if i == 1 else left}))
            sends[-1].start()

    for copy in stats + sends + swaps:
        copy.wait_send()
    for copies in parts:
        for copy in copies:
            copy.wait_send()


def merge(acc, wstat, part, pstat, w, wsib):
    bf, f32 = jnp.bfloat16, jnp.float32
    dma = pltpu.SemaphoreType.DMA
    return pl.pallas_call(
        merge_kernel,
        name="merge_and_project",
        out_shape=jax.ShapeDtypeStruct((HALF, WIDTH), bf),
        in_specs=[vmem_spec(), vmem_spec(), any_spec(), any_spec(), any_spec(), any_spec()],
        out_specs=vmem_spec(),
        scratch_shapes=[
            pltpu.VMEM((NY, QB, FEATS, BLK), bf),
            pltpu.VMEM((NY, QB, 2 * HEADS, BLK), f32),
            pltpu.VMEM((FEATS, WIDTH), bf),
            pltpu.VMEM((FEATS, WIDTH), bf),
            pltpu.VMEM((QB, BLK, FEATS), bf),
            pltpu.VMEM((QB, HALF, FEATS), bf),
            pltpu.VMEM((3, HALF, WIDTH), bf),
            pltpu.VMEM((2, HALF, WIDTH // 2), bf),
            pltpu.VMEM((2, HALF, WIDTH), bf),
            pltpu.VMEM((HALF, WIDTH), f32),
            dma((NY - 1, QB)), dma((NY - 1, QB)), dma((NY - 1,)), dma((NY - 1,)),
            dma((QB,)), dma((QB,)), dma((4,)), dma((4,)), dma((4,)),
        ],
        compiler_params=pltpu.CompilerParams(
            collective_id=1, has_side_effects=True, vmem_limit_bytes=40 * MIB
        ),
        cost_estimate=pl.CostEstimate(flops=2100 * 10**6, bytes_accessed=14 * MIB, transcendentals=0),
    )(acc, wstat, part, pstat, w, wsib)


def shards(query_rows, key_rows, value_rows, out_weight, random_ids, global_ids):
    ids = jnp.pad(random_ids, ((0, 8 - QB), (0, 128 - RAND)))
    kcol, vcol, qrow, idrow, wsib, acc, wstat = gather(query_rows, key_rows, value_rows, out_weight, ids)
    part, pstat = far(idrow, global_ids, kcol, vcol, qrow)
    return merge(acc, wstat, part, pstat, out_weight, wsib)


def solution(mesh):
    return jax.shard_map(
        shards,
        mesh=mesh,
        in_specs=(
            P("ctx", "mp"),
            P("ctx", "mp"),
            P("ctx", "mp"),
            P("mp", None),
            P("ctx", None),
            P(),
        ),
        out_specs=P(("ctx", "mp"), None),
        check_vma=False,
    )
```

time: 581 us -> 191 us (0.33)
  waiting for transfers between devices: 433 us -> 0 us
  Pallas kernels: 0 us -> 174 us
  local copies, waits for them, and re-layouts: 61 us -> 15.1 us
  matrix products: 26.3 us -> 0 us
  starting transfers between devices: 23.6 us -> 0 us
  between operations: 18.7 us -> 0.05 us
  other arithmetic: 15 us -> 0 us
    psum x1 -> x0, waiting for transfers between devices: 338 us -> none  [spread(): return lax.psum(jnp.where(mine, array, jnp.zeros_like(array)), axis)]
    pallas_call x0 -> x3, Pallas kernels: none -> 174 us  [the longest x1 93.3 us: gather(): pl.pallas_call(gather_kernel, name='gather_and_window', out_shape=(jax.Sh...]
    ppermute x2 -> x0, waiting for transfers between devices: 45.4 us -> none  [the longest x1 45.4 us: extended(): lax.ppermute(head, axis, [((i + 1) % count, i) for i in range(ends)])]
    reduce_scatter x1 -> x0, waiting for transfers between devices: 42.4 us -> none  [shards(): lax.psum_scatter(jnp.dot(attended, out_weight, preferred_element_type=jnp...]
    slice x17 -> x0, local copies, waits for them, and re-layouts: 29.7 us -> none  [the longest x10 17.8 us: block_attend(): value_heads = pair_block[..., 1, :].reshape(leading + (BLK, head_count, HD))]
    dot_general x17 -> x0, matrix products: 26.3 us -> none  [the longest x8 15.2 us: block_attend(): jnp.einsum('...qhd,...khd->...hqk', query_heads, key_heads, preferred_ele...]
    all_to_all x2 -> x0, starting transfers between devices: 17.3 us -> none  [the longest x1 12 us: shards(): lax.all_to_all(send_ids, 'ctx', split_axis=0, concat_axis=0, tiled=True)]
    gather x2 -> x0, local copies, waits for them, and re-layouts: 15.6 us -> none  [the longest x1 8.39 us: shards(): chosen = fetched.reshape((slot_total,) + fetched.shape[2:])[slot_index]]
  transfers between devices with their start and end apart: 6 -> 0, of which waited for: 4 -> 0; matrix products, arithmetic and copies ran while one was open for 6% -> 0% of each run, Pallas kernels for 0% -> 0%
where the time goes in v1:
time: 191 us; the launch traced here: 189 us
  Pallas kernels  174 us (91%)
  local copies, waits for them, and re-layouts  15.1 us (8%)
    pallas_call x1, Pallas kernels, gather(): pl.pallas_call(gather_kernel, name='gather_and_window', out_shape=(jax.Sh...  93.3 us
    pallas_call x1, Pallas kernels, merge(): pl.pallas_call(merge_kernel, name='merge_and_project', out_shape=jax.Shap...  44.5 us
    pallas_call x1, Pallas kernels, far(): pl.pallas_call(far_kernel, name='random_and_global', out_shape=(jax.Shape...  36.4 us
    unnamed x21, local copies, waits for them, and re-layouts  14.4 us

profile of v1, /device:TPU:1, one launch (start us, length us, event | category | flops | bytes accessed | tf_op | source)
XLA Modules:
  0.0 189.3 jit_solution(2667975710364318916)
XLA Ops:
  0.0 0.0 copy-start.9
  0.0 0.7 pad.4.ids_ref
  0.7 0.0 copy-start
  0.7 2.2 %copy-done = bf16[512,4096]{1,0:T(8,128)(2,1)S(1)} copy-done((bf16[512,4096]{1,0:T(8,128)(2,1)S(1)}, bf16[512,4096]{1,0:T(8,128)(2,1)}, u32[]{:S(2)}) %copy-start) | copy-done | bytes 4194328
  2.9 0.0 copy-start.6
  2.9 1.0 copy-done.6
  3.9 0.0 copy-start.7
  3.9 1.0 copy-done.7
  5.0 0.0 copy-start.8
  5.0 1.0 copy-done.8
  6.0 93.3 %gather_and_window.1 = (bf16[8,512,512]{2,1,0:T(8,128)(2,1)S(1)}, bf16[8,512,512]{2,1,0:T(8,128)(2,1)S(1)}, bf16[4,512,512]{2,1,0:T(8,128)(2,1)S(1)}, s32[4,8,12...) custom-call(bf16[512,512]{1,0:T(8,128)(2,1)S(1)} %copy-done.6, ...), custom_call_target="tpu_custom_call" | custom-call | flops 400000000 | bytes 25165824 | tf_op jit(solution)/shard_map/gather_and_window/pallas_call | solution.py:164
  99.3 0.0 copy-start.2
  99.3 1.9 %copy-done.2 = bf16[8,512,512]{2,1,0:T(8,128)(2,1)} copy-done((bf16[8,512,512]{2,1,0:T(8,128)(2,1)}, bf16[8,512,512]{2,1,0:T(8,128)(2,1)S(1)}, u32[]{:S(2)}) %copy-start.2) | copy-done | bytes 4194328
  101.3 0.0 copy-start.4
  101.3 2.0 %copy-done.4 = bf16[8,512,512]{2,1,0:T(8,128)(2,1)} copy-done((bf16[8,512,512]{2,1,0:T(8,128)(2,1)}, bf16[8,512,512]{2,1,0:T(8,128)(2,1)S(1)}, u32[]{:S(2)}) %copy-start.4) | copy-done | bytes 4194328
  103.3 0.0 copy-done.9
  103.3 0.0 copy-start.3
  103.3 2.2 %copy-done.3 = bf16[8,512,512]{2,1,0:T(8,128)(2,1)S(1)} copy-done((bf16[8,512,512]{2,1,0:T(8,128)(2,1)S(1)}, bf16[8,512,512]{2,1,0:T(8,128)(2,1)}, u32[]{:S(2)}) %copy-start.3) | copy-done | bytes 4194328
  105.4 0.0 copy-start.5
  105.4 2.2 %copy-done.5 = bf16[8,512,512]{2,1,0:T(8,128)(2,1)S(1)} copy-done((bf16[8,512,512]{2,1,0:T(8,128)(2,1)S(1)}, bf16[8,512,512]{2,1,0:T(8,128)(2,1)}, u32[]{:S(2)}) %copy-start.5) | copy-done | bytes 4194328
  107.6 0.0 copy-start.1
  107.6 36.4 %random_and_global.1 = (bf16[4,4,512,128]{3,2,1,0:T(8,128)(2,1)S(1)}, f32[4,4,8,128]{3,2,1,0:T(8,128)S(1)}) custom-call(s32[4,8,128]{2,1,0:T(8,128)S(1)} %get-tuple-element.16.ids_ref, s32[2]{0:T(128)S(1)} %copy-done.9, bf16[8,512,512]{2,1,0:T(8,128)(2,1)S(1)} %copy-done.3, bf16[8,512,512]{2,1,0:T(8,128)(2,1)S(1)} %copy-done.5, ...), custom_call_target="tpu_custom_call" | custom-call | flops 800000000 | bytes 14680064 | tf_op jit(solution)/shard_map/random_and_global/pallas_call | solution.py:239
  144.0 0.0 copy-done.1
  144.1 44.5 %merge_and_project.1 = bf16[64,4096]{1,0:T(8,128)(2,1)S(1)} custom-call(f32[4,512,128]{2,1,0:T(8,128)S(1)} %get-tuple-element.14.acc_ref, f32[4,8,128]{2,1,0:T(8,128)S(1)} %get-tuple-element.15.wstat_ref, bf16[4,4,512,128]{3,2,1,0:T(8,128)(2,1)S(1)} %get-tuple-element.20.part, f32[4,4,8,128]{3,2,1,0:T(8,128)S(1)} %get-tuple-element.21.pstat, ...), custom_call_target="tpu_custom_call" | custom-call | flops 2100000000 | bytes 14680064 | tf_op jit(solution)/shard_map/merge_and_project/pallas_call | solution.py:377
  188.5 0.8 copy.8
Async XLA Ops:
  0.0 103.3 %copy-start.9 = (s32[2]{0:T(128)S(1)}, s32[2]{0:T(128)}, u32[]{:S(2)}) copy-start(s32[2]{0:T(128)} %glob_ref.1) | copy-start | bytes 28
  0.7 2.2 %copy-start = (bf16[512,4096]{1,0:T(8,128)(2,1)S(1)}, bf16[512,4096]{1,0:T(8,128)(2,1)}, u32[]{:S(2)}) copy-start(bf16[512,4096]{1,0:T(8,128)(2,1)} %w_ref.3) | copy-start | bytes 12582916
  2.9 1.0 copy-start.6
  3.9 1.0 copy-start.7
  5.0 1.0 copy-start.8
  99.3 2.0 %copy-start.2 = (bf16[8,512,512]{2,1,0:T(8,128)(2,1)}, bf16[8,512,512]{2,1,0:T(8,128)(2,1)S(1)}, u32[]{:S(2)}) copy-start(bf16[8,512,512]{2,1,0:T(8,128)(2,1)S(1)} %get-tuple-element.17.kcol) | copy-start | bytes 12582916
  101.3 2.0 %copy-start.4 = (bf16[8,512,512]{2,1,0:T(8,128)(2,1)}, bf16[8,512,512]{2,1,0:T(8,128)(2,1)S(1)}, u32[]{:S(2)}) copy-start(bf16[8,512,512]{2,1,0:T(8,128)(2,1)S(1)} %get-tuple-element.18.vcol) | copy-start | bytes 12582916
  103.3 2.2 %copy-start.3 = (bf16[8,512,512]{2,1,0:T(8,128)(2,1)S(1)}, bf16[8,512,512]{2,1,0:T(8,128)(2,1)}, u32[]{:S(2)}) copy-start(bf16[8,512,512]{2,1,0:T(8,128)(2,1)} %copy-done.2) | copy-start | bytes 12582916
  105.4 2.2 %copy-start.5 = (bf16[8,512,512]{2,1,0:T(8,128)(2,1)S(1)}, bf16[8,512,512]{2,1,0:T(8,128)(2,1)}, u32[]{:S(2)}) copy-start(bf16[8,512,512]{2,1,0:T(8,128)(2,1)} %copy-done.4) | copy-start | bytes 12582916
  107.6 36.4 %copy-start.1 = (bf16[512,4096]{1,0:T(8,128)(2,1)S(1)}, bf16[512,4096]{1,0:T(8,128)(2,1)}, u32[]{:S(2)}) copy-start(bf16[512,4096]{1,0:T(8,128)(2,1)} %w_ref.3) | copy-start | bytes 12582916

commit v2 on v0

v2 whole, which is shorter than its diff:
```python
import math

import jax
import jax.numpy as jnp
from jax import lax
from jax.experimental import pallas as pl
from jax.experimental.pallas import tpu as pltpu
from jax.sharding import PartitionSpec as P

HD = 128
BLK = 128
RAND = 3
GLOB = 2
CAND = GLOB + RAND
NZ = 8
NY = 4
NX = 4
HEADS = 4
PAIR = 2 * HD
QB = 4
FEATS = HEADS * HD
WIDTH = 4096
HALF = BLK // 2
TILE = 512
SCALE = 1.0 / math.sqrt(HD)
LOW = -1e30
MESH = pl.DeviceIdType.MESH
NT = (((1,), (1,)), ((), ()))
RING = 28
MIB = 1024 * 1024


def kernel(
    q_ref, k_ref, v_ref, w_ref, ids_ref, glob_ref, out_ref,
    k_col, v_col0, v_col1, q_row, id_row, id_s, k_ext, v_ext, v_own, acc, w_stat,
    probs, part, p_stat, got, got_stat, w_own, w_other, att, att_other, sent, relay, final, total,
    ring_send, ring_recv, row_send, row_recv, edge_send, edge_recv, w_sem, local_sem,
    part_send, part_recv, stat_send, stat_recv, att_send, att_recv, x_send, x_recv,
):
    me, mp = lax.axis_index("ctx"), lax.axis_index("mp")
    z, y, x, core = me // NY, me % NY, mp // 2, mp % 2
    count = NZ * NY
    after, before = (me + 1) % count, (me + count - 1) % count
    sibling = mp + 1 - 2 * core
    up, down = (z + 1) % NZ, (z + NZ - 1) % NZ
    right, left = ((x + 1) % NX) * 2 + core, ((x + NX - 1) % NX) * 2 + core
    order = [(x + d) % NX for d in (2, 1, 3, 0)]
    v_cols = (v_col0, v_col1)

    local = [
        pltpu.make_async_copy(v_ref, v_own, local_sem.at[0]),
        pltpu.make_async_copy(q_ref, q_row.at[pl.ds(y * QB, QB)], local_sem.at[1]),
        pltpu.make_async_copy(k_ref, k_ext.at[pl.ds(1, QB)], local_sem.at[2]),
        pltpu.make_async_copy(k_ref, k_col.at[pl.ds(z * QB, QB)], local_sem.at[3]),
        pltpu.make_async_copy(ids_ref, id_row.at[y], local_sem.at[4]),
        pltpu.make_async_copy(w_ref, w_own, local_sem.at[5]),
    ]
    for copy in local:
        copy.start()

    barrier = pltpu.get_barrier_semaphore()
    peers = [{"ctx": up * NY + y}, {"ctx": down * NY + y}]
    peers += [{"ctx": z * NY + (y + d) % NY} for d in range(1, NY)]
    peers += [{"ctx": after}, {"ctx": before}, {"mp": sibling}, {"mp": right}, {"mp": left}]
    for peer in peers:
        pl.semaphore_signal(barrier, inc=1, device_id=peer, device_id_type=MESH)
    pl.semaphore_wait(barrier, len(peers))

    def remote(src, dst, send, recv, peer):
        return pltpu.make_async_remote_copy(
            src_ref=src, dst_ref=dst, send_sem=send, recv_sem=recv, device_id=peer, device_id_type=MESH
        )

    def ring(way, i):
        sign = 1 if way == 0 else -1
        peer = {"ctx": (up if way == 0 else down) * NY + y}
        sems = (ring_send.at[way, i], ring_recv.at[way, i])
        if i < 14:
            back, piece = i // 4, (i % 4 + 2 * way) % 4
            first = ((z + NZ - sign * back) % NZ) * QB
            src = k_ref.at[piece] if back == 0 else k_col.at[first + piece]
            return remote(src, k_col.at[first + piece], *sems, peer)
        heads, j = (i - 14) // 7, (i - 14) % 7
        back, piece = j // 2, (j % 2 + way) % 2
        first = ((z + NZ - sign * back) % NZ) * QB
        span = v_cols[heads].at[pl.ds(first + 2 * piece, 2)]
        return remote(span, span, *sems, peer)

    rings = [[ring(way, i) for i in range(RING)] for way in range(2)]
    follow = {r: [r + 4] for r in range(10)}
    follow[9] += [14, 15]
    for start in (14, 21):
        for r in range(start, start + 5):
            follow[r] = [r + 2]
    follow[18] += [21, 22]

    def advance(r):
        for way in range(2):
            rings[way][r].wait_recv()
            for s in follow.get(r, ()):
                rings[way][s].start()

    for i in range(4):
        rings[0][i].start()
        rings[1][i].start()
    edges = [
        remote(k_ref.at[QB - 1], k_ext.at[0], edge_send.at[0], edge_recv.at[0], {"ctx": after}),
        remote(k_ref.at[0], k_ext.at[QB + 1], edge_send.at[1], edge_recv.at[1], {"ctx": before}),
        remote(v_ext.at[QB], v_ext.at[0], edge_send.at[2], edge_recv.at[2], {"ctx": after}),
        remote(v_ext.at[1], v_ext.at[QB + 1], edge_send.at[3], edge_recv.at[3], {"ctx": before}),
    ]
    edges[0].start()
    edges[1].start()
    rows = []
    for d in range(1, NY):
        peer = {"ctx": z * NY + (y + d) % NY}
        rows.append(remote(ids_ref, id_row.at[y], row_send.at[1, d - 1], row_recv.at[1, d - 1], peer))
        rows.append(remote(q_ref, q_row.at[pl.ds(y * QB, QB)], row_send.at[0, d - 1], row_recv.at[0, d - 1], peer))
    for copy in rows:
        copy.start()
    weight = remote(w_ref, w_other, w_sem.at[0], w_sem.at[1], {"mp": sibling})
    weight.start()

    local[0].wait()

    def turn(b, carry):
        for h in range(HEADS):
            flipped = v_own[b, :, pl.ds(h * HD, HD)].T
            v_ext[b + 1, pl.ds(h * HD, HD), :] = flipped
            v_cols[h // 2][z * QB + b, pl.ds((h % 2) * HD, HD), :] = flipped
        return carry

    lax.fori_loop(0, QB, turn, 0)
    edges[2].start()
    edges[3].start()
    advance(0)
    for copy in local[1:]:
        copy.wait()
    for copy in edges:
        copy.wait_recv()

    def window(qb):
        row = lax.broadcasted_iota(jnp.int32, (3 * BLK, 1), 0)
        first = jnp.where(me + qb == 0, BLK, 0)
        last = jnp.where(me * QB + qb == count * QB - 1, 2 * BLK, 3 * BLK)
        live = (row >= first) & (row < last)
        for h in range(HEADS):
            cols = pl.ds(h * HD, HD)
            keys = jnp.concatenate([k_ext[qb + j, :, cols] for j in range(3)], axis=0)
            values = jnp.concatenate([v_ext[qb + j, cols, :] for j in range(3)], axis=1)
            s = lax.dot_general(keys, q_row[y * QB + qb, :, cols], NT, preferred_element_type=jnp.float32) * SCALE
            s = jnp.where(live, s, LOW)
            top = jnp.max(s, axis=0, keepdims=True)
            p = jnp.exp(s - top).astype(jnp.bfloat16)
            w_stat[qb, pl.ds(h, 1), :] = top
            w_stat[qb, pl.ds(HEADS + h, 1), :] = jnp.sum(p.astype(jnp.float32), axis=0, keepdims=True)
            acc[qb, cols, :] = jnp.dot(values, p, preferred_element_type=jnp.float32)

    for r in range(1, 10):
        if r <= QB:
            window(r - 1)
        advance(r)

    for copy in rows:
        copy.wait_recv()
    to_scalar = pltpu.make_async_copy(id_row, id_s, local_sem.at[6])
    to_scalar.start()
    to_scalar.wait()
    for r in range(10, 14):
        advance(r)

    def candidates(t):
        blocks = [glob_ref[j] for j in range(GLOB)]
        blocks += [id_s[lax.div(t, QB), lax.rem(t, QB), j] for j in range(RAND)]
        spots = [lax.div(block, NY * QB) * QB + lax.rem(block, QB) for block in blocks]
        return blocks, spots

    def score(t, carry):
        blocks, spots = candidates(t)
        bias = [jnp.where(lax.rem(lax.div(block, QB), NY) == y, 0.0, LOW) for block in blocks]
        for h in range(HEADS):
            cols = pl.ds(h * HD, HD)
            keys = jnp.concatenate([k_col[spot, :, cols] for spot in spots], axis=0)
            s = lax.dot_general(keys, q_row[t, :, cols], NT, preferred_element_type=jnp.float32)
            s = jnp.concatenate([s[j * BLK:(j + 1) * BLK] * SCALE + bias[j] for j in range(CAND)], axis=0)
            top = jnp.max(s, axis=0, keepdims=True)
            p = jnp.exp(s - top).astype(jnp.bfloat16)
            p_stat[t, pl.ds(h, 1), :] = top
            p_stat[t, pl.ds(HEADS + h, 1), :] = jnp.sum(p.astype(jnp.float32), axis=0, keepdims=True)
            probs[t, h] = p
        return carry

    steps = [0, 3, 6, 9, 12, 14, 16]
    for n, r in enumerate(range(14, 20)):
        lax.fori_loop(steps[n], steps[n + 1], score, 0)
        advance(r)

    stats = []
    for d in range(1, NY):
        to = (y + d) % NY
        stats.append(remote(p_stat.at[pl.ds(to * QB, QB)], got_stat.at[d - 1], stat_send.at[d - 1],
                            stat_recv.at[d - 1], {"ctx": z * NY + to}))
        stats[-1].start()
    advance(20)

    def returns(pair, i):
        qb = order[i]
        span = pl.ds(pair * PAIR, PAIR)
        copies = []
        for d in (2, 1, 3):
            to = (y + d) % NY
            copies.append(remote(part.at[to * QB + qb, span], got.at[d - 1, qb, span],
                                 part_send.at[pair, d - 1, i], part_recv.at[pair, d - 1, i], {"ctx": z * NY + to}))
        return copies

    def weigh(pair, i):
        qb = order[i]

        def one(to, carry):
            t = to * QB + qb
            spots = candidates(t)[1]
            for g in range(2):
                h = 2 * pair + g
                values = jnp.concatenate([v_cols[pair][spot, pl.ds(g * HD, HD), :] for spot in spots], axis=1)
                out = jnp.dot(values, probs[t, h], preferred_element_type=jnp.float32)
                out = out / p_stat[t, pl.ds(HEADS + h, 1), :]
                part[t, pl.ds(h * HD, HD), :] = out.astype(jnp.bfloat16)
            return carry

        lax.fori_loop(0, NY, one, 0)

    def merge(pair, i):
        qb = order[i]
        for g in range(2):
            h = 2 * pair + g
            cols = pl.ds(h * HD, HD)
            line, low_line = pl.ds(h, 1), pl.ds(HEADS + h, 1)
            tops = [w_stat[qb, line, :], p_stat[y * QB + qb, line, :]]
            tops += [got_stat[s, qb, line, :] for s in range(NY - 1)]
            sums = [w_stat[qb, low_line, :], p_stat[y * QB + qb, low_line, :]]
            sums += [got_stat[s, qb, low_line, :] for s in range(NY - 1)]
            best = tops[0]
            for top in tops[1:]:
                best = jnp.maximum(best, top)
            scales = [jnp.exp(top - best) for top in tops]
            weights = [scale * total_of for scale, total_of in zip(scales, sums)]
            low = weights[0] + weights[1] + weights[2] + weights[3] + weights[4]
            value = acc[qb, cols, :] * (scales[0] / low)
            value += part[y * QB + qb, cols, :].astype(jnp.float32) * (weights[1] / low)
            for s in range(NY - 1):
                value += got[s, qb, cols, :].astype(jnp.float32) * (weights[s + 2] / low)
            att[i, :, cols] = value.T.astype(jnp.bfloat16)

    parts = [[returns(pair, i) for i in range(QB)] for pair in range(2)]
    for i in range(QB):
        weigh(0, i)
        for copy in parts[0][i]:
            copy.start()
        advance(21 + i)
    for copy in stats:
        copy.wait_recv()
    weight.wait()
    for n, r in enumerate((25, 26)):
        for i in (2 * n, 2 * n + 1):
            for copy in parts[0][i]:
                copy.wait_recv()
            merge(0, i)
        advance(r)
    advance(27)

    for i in range(QB):
        weigh(1, i)
        for copy in parts[1][i]:
            copy.start()

    swaps, sends = [], []
    mine = pl.ds(pl.multiple_of(core * HALF, HALF), HALF)
    theirs = pl.ds(pl.multiple_of((1 - core) * HALF, HALF), HALF)
    middle = WIDTH // 2
    for i in range(QB):
        for copy in parts[1][i]:
            copy.wait_recv()
        merge(1, i)
        swaps.append(remote(att.at[i, theirs], att_other.at[i], att_send.at[i], att_recv.at[i], {"mp": sibling}))
        swaps[i].start()

        def own(n, carry):
            cols = pl.ds(pl.multiple_of(n * TILE, TILE), TILE)
            total[:, cols] = jnp.dot(att[i, mine, :], w_own[:, cols], preferred_element_type=jnp.float32)
            return carry

        lax.fori_loop(0, WIDTH // TILE, own, 0)
        swaps[i].wait_recv()
        if 1 <= i < 3:
            sends[i - 1].wait_recv()
        if i == 3:
            sends[2].wait_recv()
            sends[3].wait_recv()

        def other(n, carry):
            cols = pl.ds(pl.multiple_of(n * TILE, TILE), TILE)
            value = total[:, cols] + jnp.dot(att_other[i], w_other[:, cols], preferred_element_type=jnp.float32)
            if i == 3:
                value += final[0, :, cols].astype(jnp.float32) + final[1, :, cols].astype(jnp.float32)
                out_ref[:, cols] = value.astype(jnp.bfloat16)
            else:
                sent[i, :, cols] = value.astype(jnp.bfloat16)
            return carry

        def other_relay(n, carry):
            place = n * TILE + (i - 1) * middle
            cols = pl.ds(pl.multiple_of(place, TILE), TILE)
            near = pl.ds(pl.multiple_of(n * TILE, TILE), TILE)
            value = total[:, cols] + jnp.dot(att_other[i], w_other[:, cols], preferred_element_type=jnp.float32)
            sent[i, :, cols] = (value + relay[i - 1, :, near].astype(jnp.float32)).astype(jnp.bfloat16)
            return carry

        tiles = WIDTH // TILE
        if i == 1:
            lax.fori_loop(tiles // 2, tiles, other, 0)
            lax.fori_loop(0, tiles // 2, other_relay, 0)
        elif i == 2:
            lax.fori_loop(0, tiles // 2, other, 0)
            lax.fori_loop(0, tiles // 2, other_relay, 0)
        else:
            lax.fori_loop(0, tiles, other, 0)
        if i == 0:
            for s, peer in enumerate((right, left)):
                sends.append(remote(sent.at[0, :, pl.ds(s * middle, middle)], relay.at[s],
                                    x_send.at[s], x_recv.at[s], {"mp": peer}))
                sends[-1].start()
        elif i < 3:
            sends.append(remote(sent.at[i], final.at[i - 1], x_send.at[i + 1], x_recv.at[i + 1],
                                {"mp": right if i == 1 else left}))
            sends[-1].start()

    for copy in edges + rings[0] + rings[1] + rows + stats + swaps + sends:
        copy.wait_send()
    for copies in parts[0] + parts[1]:
        for copy in copies:
            copy.wait_send()


def shards(query_rows, key_rows, value_rows, out_weight, random_ids, global_ids):
    bf, f32 = jnp.bfloat16, jnp.float32
    dma = pltpu.SemaphoreType.DMA
    vmem = pltpu.VMEM
    ids = jnp.pad(random_ids, ((0, 8 - QB), (0, 128 - RAND)))
    anywhere = pl.BlockSpec(memory_space=pl.ANY)
    blocks = (QB, BLK, FEATS)
    return pl.pallas_call(
        kernel,
        name="attend_and_project",
        out_shape=jax.ShapeDtypeStruct((HALF, WIDTH), bf),
        in_specs=[anywhere] * 5 + [pl.BlockSpec(memory_space=pltpu.SMEM)],
        out_specs=pl.BlockSpec(memory_space=pltpu.VMEM),
        scratch_shapes=[
            vmem((NZ * QB, BLK, FEATS), bf),
            vmem((NZ * QB, PAIR, BLK), bf),
            vmem((NZ * QB, PAIR, BLK), bf),
            vmem((NY * QB, BLK, FEATS), bf),
            vmem((NY, 8, 128), jnp.int32),
            pltpu.SMEM((NY, 8, 128), jnp.int32),
            vmem((QB + 2, BLK, FEATS), bf),
            vmem((QB + 2, FEATS, BLK), bf),
            vmem(blocks, bf),
            vmem((QB, FEATS, BLK), f32),
            vmem((QB, 2 * HEADS, BLK), f32),
            vmem((NY * QB, HEADS, CAND * BLK, BLK), bf),
            vmem((NY * QB, FEATS, BLK), bf),
            vmem((NY * QB, 2 * HEADS, BLK), f32),
            vmem((NY - 1, QB, FEATS, BLK), bf),
            vmem((NY - 1, QB, 2 * HEADS, BLK), f32),
            vmem((FEATS, WIDTH), bf),
            vmem((FEATS, WIDTH), bf),
            vmem((QB, BLK, FEATS), bf),
            vmem((QB, HALF, FEATS), bf),
            vmem((3, HALF, WIDTH), bf),
            vmem((2, HALF, WIDTH // 2), bf),
            vmem((2, HALF, WIDTH), bf),
            vmem((HALF, WIDTH), f32),
            dma((2, RING)), dma((2, RING)), dma((2, NY - 1)), dma((2, NY - 1)),
            dma((4,)), dma((4,)), dma((2,)), dma((7,)),
            dma((2, NY - 1, QB)), dma((2, NY - 1, QB)), dma((NY - 1,)), dma((NY - 1,)),
            dma((QB,)), dma((QB,)), dma((4,)), dma((4,)),
        ],
        compiler_params=pltpu.CompilerParams(
            collective_id=0, has_side_effects=True, vmem_limit_bytes=56 * MIB
        ),
        cost_estimate=pl.CostEstimate(flops=4 * 10**9, bytes_accessed=24 * MIB, transcendentals=0),
    )(
        query_rows.reshape(blocks), key_rows.reshape(blocks), value_rows.reshape(blocks),
        out_weight, ids, global_ids,
    )


def solution(mesh):
    return jax.shard_map(
        shards,
        mesh=mesh,
        in_specs=(
            P("ctx", "mp"),
            P("ctx", "mp"),
            P("ctx", "mp"),
            P("mp", None),
            P("ctx", None),
            P(),
        ),
        out_specs=P(("ctx", "mp"), None),
        check_vma=False,
    )
```

time: 581 us -> 152 us (0.26)
  waiting for transfers between devices: 433 us -> 0 us
  Pallas kernels: 0 us -> 148 us
  local copies, waits for them, and re-layouts: 61 us -> 3.15 us
  matrix products: 26.3 us -> 0 us
  starting transfers between devices: 23.6 us -> 0 us
  between operations: 18.7 us -> 0.01 us
  other arithmetic: 15 us -> 0 us
    psum x1 -> x0, waiting for transfers between devices: 338 us -> none  [spread(): return lax.psum(jnp.where(mine, array, jnp.zeros_like(array)), axis)]
    pallas_call x0 -> x1, Pallas kernels: none -> 148 us  [shards(): pl.pallas_call(kernel, name='attend_and_project', out_shape=jax.ShapeDtyp...]
    ppermute x2 -> x0, waiting for transfers between devices: 45.4 us -> none  [the longest x1 45.4 us: extended(): lax.ppermute(head, axis, [((i + 1) % count, i) for i in range(ends)])]
    reduce_scatter x1 -> x0, waiting for transfers between devices: 42.4 us -> none  [shards(): lax.psum_scatter(jnp.dot(attended, out_weight, preferred_element_type=jnp...]
    slice x17 -> x0, local copies, waits for them, and re-layouts: 29.7 us -> none  [the longest x10 17.8 us: block_attend(): value_heads = pair_block[..., 1, :].reshape(leading + (BLK, head_count, HD))]
    dot_general x17 -> x0, matrix products: 26.3 us -> none  [the longest x8 15.2 us: block_attend(): jnp.einsum('...qhd,...khd->...hqk', query_heads, key_heads, preferred_ele...]
    all_to_all x2 -> x0, starting transfers between devices: 17.3 us -> none  [the longest x1 12 us: shards(): lax.all_to_all(send_ids, 'ctx', split_axis=0, concat_axis=0, tiled=True)]
    gather x2 -> x0, local copies, waits for them, and re-layouts: 15.6 us -> none  [the longest x1 8.39 us: shards(): chosen = fetched.reshape((slot_total,) + fetched.shape[2:])[slot_index]]
  transfers between devices with their start and end apart: 6 -> 0, of which waited for: 4 -> 0; matrix products, arithmetic and copies ran while one was open for 6% -> 0% of each run, Pallas kernels for 0% -> 0%
where the time goes in v2:
time: 152 us
  Pallas kernels  148 us (97%)
  local copies, waits for them, and re-layouts  3.15 us (2%)
    pallas_call x1, Pallas kernels, shards(): pl.pallas_call(kernel, name='attend_and_project', out_shape=jax.ShapeDtyp...  148 us

profile of v2, /device:TPU:1, one launch (start us, length us, event | category | flops | bytes accessed | tf_op | source)
XLA Modules:
  0.0 151.7 jit_solution(4203011257359088908)
XLA Ops:
  0.0 1.3 pad.4.ids_ref
  1.3 148.5 %attend_and_project.1 = bf16[64,4096]{1,0:T(8,128)(2,1)} custom-call(bf16[4,128,512]{2,1,0:T(8,128)(2,1)} %bitcast.3, bf16[4,128,512]{2,1,0:T(8,128)(2,1)} %bitcast.4, bf16[4,128,512]{2,1,0:T(8,128)(2,1)} %bitcast.5, bf16[512,4096]{1,0:T(8,128)(2,1)} %w_ref.1, s32[8,128]{1,0:T(8,128)} %pad.4.ids_ref, s32[2]{0:T(128)} %glob_ref.1), custom_call_target="tpu_custom_call" | custom-call | flops 4000000000 | bytes 25165824 | tf_op jit(solution)/shard_map/attend_and_project/pallas_call | solution.py:351
  149.8 1.9 %copy.8 = bf16[64,4096]{1,0:T(8,128)(2,1)} copy(bf16[64,4096]{1,0:T(8,128)(2,1)} %attend_and_project.1) | data formatting | bytes 1048576

commit v3 on v2

v3 whole, which is shorter than its diff:
```python
import math

import jax
import jax.numpy as jnp
from jax import lax
from jax.experimental import pallas as pl
from jax.experimental.pallas import tpu as pltpu
from jax.sharding import PartitionSpec as P

HD = 128
BLK = 128
RAND = 3
GLOB = 2
CAND = GLOB + RAND
NZ = 8
NY = 4
NX = 4
HEADS = 4
QB = 4
FEATS = HEADS * HD
WIDTH = 4096
HALF = BLK // 2
TILE = 512
SCALE = 1.0 / math.sqrt(HD)
LOW = -1e30
MESH = pl.DeviceIdType.MESH
NT = (((1,), (1,)), ((), ()))
PHASES = 1 + HEADS
TILES = WIDTH // TILE
MIDDLE = WIDTH // 2
MIB = 1024 * 1024


def ring_order():
    order = [(0, 0, j) for j in range(4)]
    for p in range(PHASES):
        ahead = [(p + 1, 0, j) for j in range(4)] if p + 1 < PHASES else []
        order += [(p, 1, j) for j in range(4)] + ahead[:2]
        order += [(p, 2, j) for j in range(4)] + ahead[2:]
        order += [(p, 3, j) for j in range(2)]
    return order


ORDER = ring_order()
RING = len(ORDER)
SPOT = {item: n for n, item in enumerate(ORDER)}
DONE = [SPOT[p, 3, 1] for p in range(PHASES)]


def followers():
    follow, last = {}, -1
    for n, (p, back, j) in enumerate(ORDER):
        if back > 0:
            last = max(last, SPOT[p, back - 1, j])
        follow.setdefault(last, []).append(n)
    return follow


def kernel(
    q_ref, k_ref, v_ref, w_ref, ids_ref, glob_ref, out_ref,
    k_col, v_col0, v_col1, v_col2, v_col3, q_row, id_row, id_s, k_edge, v_edge, v_own, acc, w_stat, w_probs,
    probs, part, p_stat, got, got_stat, w_own, w_other, att, att_other, sent, relay, final, total,
    ring_send, ring_recv, row_send, row_recv, id_send, id_recv, edge_send, edge_recv, w_sem, local_sem,
    part_send, part_recv, stat_send, stat_recv, att_send, att_recv, x_send, x_recv,
):
    me, mp = lax.axis_index("ctx"), lax.axis_index("mp")
    z, y, x, core = me // NY, me % NY, mp // 2, mp % 2
    count = NZ * NY
    sibling = mp + 1 - 2 * core
    up, down = (z + 1) % NZ, (z + NZ - 1) % NZ
    right, left = ((x + 1) % NX) * 2 + core, ((x + NX - 1) % NX) * 2 + core
    order = [(x + d) % NX for d in (2, 1, 3, 0)]
    v_cols = (v_col0, v_col1, v_col2, v_col3)

    local = [
        pltpu.make_async_copy(v_ref, v_own, local_sem.at[0]),
        pltpu.make_async_copy(q_ref, q_row.at[pl.ds(y * QB, QB)], local_sem.at[1]),
        pltpu.make_async_copy(k_ref, k_col.at[pl.ds(z * QB, QB)], local_sem.at[2]),
        pltpu.make_async_copy(ids_ref, id_row.at[y], local_sem.at[3]),
        pltpu.make_async_copy(w_ref, w_own, local_sem.at[4]),
    ]
    for copy in local:
        copy.start()

    barrier = pltpu.get_barrier_semaphore()
    peers = [{"ctx": up * NY + y}, {"ctx": down * NY + y}]
    peers += [{"ctx": z * NY + (y + d) % NY} for d in range(1, NY)]
    peers += [{"mp": sibling}, {"mp": right}, {"mp": left}]
    for peer in peers:
        pl.semaphore_signal(barrier, inc=1, device_id=peer, device_id_type=MESH)
    pl.semaphore_wait(barrier, len(peers))

    def remote(src, dst, send, recv, peer):
        return pltpu.make_async_remote_copy(
            src_ref=src, dst_ref=dst, send_sem=send, recv_sem=recv, device_id=peer, device_id_type=MESH
        )

    def ring(way, n):
        p, back, j = ORDER[n]
        sign = 1 if way == 0 else -1
        peer = {"ctx": (up if way == 0 else down) * NY + y}
        sems = (ring_send.at[way, n], ring_recv.at[way, n])
        piece = (j + 2 * way) % 4
        block = ((z + NZ - sign * back) % NZ) * QB + piece
        if p > 0:
            return remote(v_cols[p - 1].at[block], v_cols[p - 1].at[block], *sems, peer)
        return remote(k_ref.at[piece] if back == 0 else k_col.at[block], k_col.at[block], *sems, peer)

    rings = [[ring(way, n) for n in range(RING)] for way in range(2)]
    follow = followers()
    for n in follow[-1]:
        rings[0][n].start()
        rings[1][n].start()

    above = jnp.where(y < NY - 1, z, down) * QB + QB - 1
    below = jnp.where(y > 0, z, up) * QB
    next_y, last_y = {"ctx": z * NY + (y + 1) % NY}, {"ctx": z * NY + (y + NY - 1) % NY}
    edges = []
    for p in range(PHASES):
        source = k_col if p == 0 else v_cols[p - 1]
        target = k_edge if p == 0 else v_edge
        spots = (0, 1) if p == 0 else (2 * p - 2, 2 * p - 1)
        edges.append([
            remote(source.at[above], target.at[spots[0]], edge_send.at[p, 0], edge_recv.at[p, 0], next_y),
            remote(source.at[below], target.at[spots[1]], edge_send.at[p, 1], edge_recv.at[p, 1], last_y),
        ])
    numbers, rows = [], []
    for d in range(1, NY):
        peer = {"ctx": z * NY + (y + d) % NY}
        numbers.append(remote(ids_ref, id_row.at[y], id_send.at[d - 1], id_recv.at[d - 1], peer))
        for b in range(QB):
            rows.append(remote(q_ref.at[b], q_row.at[y * QB + b], row_send.at[d - 1, b], row_recv.at[d - 1, b], peer))
    for copy in numbers:
        copy.start()
    weight = remote(w_ref, w_other, w_sem.at[0], w_sem.at[1], {"mp": sibling})
    weight.start()

    local[0].wait()

    def turn(b, carry):
        for h in range(HEADS):
            v_cols[h][z * QB + b] = v_own[b, :, pl.ds(h * HD, HD)].T
        return carry

    lax.fori_loop(0, QB, turn, 0)
    for copy in local[1:]:
        copy.wait()

    def window_score(qb):
        row = lax.broadcasted_iota(jnp.int32, (3 * BLK, 1), 0)
        first = jnp.where(me + qb == 0, BLK, 0)
        last = jnp.where(me * QB + qb == count * QB - 1, 2 * BLK, 3 * BLK)
        live = (row >= first) & (row < last)
        for h in range(HEADS):
            cols = pl.ds(h * HD, HD)
            keys = [k_edge[0, :, cols] if qb == 0 else k_col[z * QB + qb - 1, :, cols]]
            keys.append(k_col[z * QB + qb, :, cols])
            keys.append(k_edge[1, :, cols] if qb == QB - 1 else k_col[z * QB + qb + 1, :, cols])
            s = lax.dot_general(jnp.concatenate(keys, axis=0), q_row[y * QB + qb, :, cols], NT,
                                preferred_element_type=jnp.float32) * SCALE
            s = jnp.where(live, s, LOW)
            top = jnp.max(s, axis=0, keepdims=True)
            p = jnp.exp(s - top).astype(jnp.bfloat16)
            w_stat[qb, pl.ds(h, 1), :] = top
            w_stat[qb, pl.ds(HEADS + h, 1), :] = jnp.sum(p.astype(jnp.float32), axis=0, keepdims=True)
            w_probs[qb, h] = p

    def window_weigh(h):
        for copy in edges[h + 1]:
            copy.wait_recv()
        for qb in range(QB):
            values = [v_edge[2 * h] if qb == 0 else v_cols[h][z * QB + qb - 1]]
            values.append(v_cols[h][z * QB + qb])
            values.append(v_edge[2 * h + 1] if qb == QB - 1 else v_cols[h][z * QB + qb + 1])
            acc[qb, pl.ds(h * HD, HD), :] = jnp.dot(
                jnp.concatenate(values, axis=1), w_probs[qb, h], preferred_element_type=jnp.float32)

    def candidates(t):
        blocks = [glob_ref[j] for j in range(GLOB)]
        blocks += [id_s[lax.div(t, QB), lax.rem(t, QB), j] for j in range(RAND)]
        spots = [lax.div(block, NY * QB) * QB + lax.rem(block, QB) for block in blocks]
        return blocks, spots

    def score(t, carry):
        blocks, spots = candidates(t)
        bias = [jnp.where(lax.rem(lax.div(block, QB), NY) == y, 0.0, LOW) for block in blocks]
        for h in range(HEADS):
            cols = pl.ds(h * HD, HD)
            keys = jnp.concatenate([k_col[spot, :, cols] for spot in spots], axis=0)
            s = lax.dot_general(keys, q_row[t, :, cols], NT, preferred_element_type=jnp.float32)
            s = jnp.concatenate([s[j * BLK:(j + 1) * BLK] * SCALE + bias[j] for j in range(CAND)], axis=0)
            top = jnp.max(s, axis=0, keepdims=True)
            p = jnp.exp(s - top).astype(jnp.bfloat16)
            p_stat[t, pl.ds(h, 1), :] = top
            p_stat[t, pl.ds(HEADS + h, 1), :] = jnp.sum(p.astype(jnp.float32), axis=0, keepdims=True)
            probs[t, h] = p
        return carry

    stats = []
    for d in range(1, NY):
        to = (y + d) % NY
        stats.append(remote(p_stat.at[pl.ds(to * QB, QB)], got_stat.at[d - 1], stat_send.at[d - 1],
                            stat_recv.at[d - 1], {"ctx": z * NY + to}))

    def returns(h, i):
        span = pl.ds(h * HD, HD)
        copies = []
        for d in (2, 1, 3):
            to = (y + d) % NY
            copies.append(remote(part.at[to * QB + order[i], span], got.at[d - 1, order[i], span],
                                 part_send.at[h, d - 1, i], part_recv.at[h, d - 1, i], {"ctx": z * NY + to}))
        return copies

    parts = [[returns(h, i) for i in range(QB)] for h in range(HEADS)]

    def weigh(h, i):
        def one(to, carry):
            t = to * QB + order[i]
            spots = candidates(t)[1]
            values = jnp.concatenate([v_cols[h][spot] for spot in spots], axis=1)
            out = jnp.dot(values, probs[t, h], preferred_element_type=jnp.float32)
            out = out / p_stat[t, pl.ds(HEADS + h, 1), :]
            part[t, pl.ds(h * HD, HD), :] = out.astype(jnp.bfloat16)
            return carry

        lax.fori_loop(0, NY, one, 0)
        for copy in parts[h][i]:
            copy.start()

    def merge(h, i):
        for copy in parts[h][i]:
            copy.wait_recv()
        qb = order[i]
        cols = pl.ds(h * HD, HD)
        line, low_line = pl.ds(h, 1), pl.ds(HEADS + h, 1)
        tops = [w_stat[qb, line, :], p_stat[y * QB + qb, line, :]]
        tops += [got_stat[s, qb, line, :] for s in range(NY - 1)]
        sums = [w_stat[qb, low_line, :], p_stat[y * QB + qb, low_line, :]]
        sums += [got_stat[s, qb, low_line, :] for s in range(NY - 1)]
        best = tops[0]
        for top in tops[1:]:
            best = jnp.maximum(best, top)
        scales = [jnp.exp(top - best) for top in tops]
        weights = [scale * total_of for scale, total_of in zip(scales, sums)]
        low = weights[0] + weights[1] + weights[2] + weights[3] + weights[4]
        value = acc[qb, cols, :] * (scales[0] / low)
        value += part[y * QB + qb, cols, :].astype(jnp.float32) * (weights[1] / low)
        for s in range(NY - 1):
            value += got[s, qb, cols, :].astype(jnp.float32) * (weights[s + 2] / low)
        att[i, :, cols] = value.T.astype(jnp.bfloat16)

    mine = pl.ds(pl.multiple_of(core * HALF, HALF), HALF)
    theirs = pl.ds(pl.multiple_of((1 - core) * HALF, HALF), HALF)
    early, late = pl.ds(0, 2 * HD), pl.ds(2 * HD, 2 * HD)
    swaps = [[remote(att.at[i, theirs, cols], att_other.at[i, :, cols], att_send.at[n, i], att_recv.at[n, i],
                     {"mp": sibling}) for i in range(QB)] for n, cols in enumerate((early, late))]

    def project_early(n, carry):
        cols = pl.ds(pl.multiple_of(n * TILE, TILE), TILE)
        own = jnp.concatenate([att[i, mine, early] for i in range(QB)], axis=0)
        other = jnp.concatenate([att_other[i, :, early] for i in range(QB)], axis=0)
        value = jnp.dot(own, w_own[early, cols], preferred_element_type=jnp.float32)
        value += jnp.dot(other, w_other[early, cols], preferred_element_type=jnp.float32)
        for i in range(QB):
            total[i, :, cols] = value[i * HALF:(i + 1) * HALF]
        return carry

    work = {}

    def at(r, *calls):
        work.setdefault(r, []).extend(calls)

    def edges_go(p):
        for copy in edges[p]:
            copy.start()

    def edges_come():
        for copy in edges[0]:
            copy.wait_recv()

    def rows_come():
        for copy in rows + numbers:
            copy.wait_recv()
        to_scalar = pltpu.make_async_copy(id_row, id_s, local_sem.at[5])
        to_scalar.start()
        to_scalar.wait()

    def stats_go():
        for copy in stats:
            copy.start()

    def stats_come():
        for copy in stats:
            copy.wait_recv()

    def swaps_go():
        for copy in swaps[0]:
            copy.start()

    def swaps_come():
        for copy in swaps[0]:
            copy.wait_recv()
        weight.wait()

    for n, b in enumerate([d * QB + b for b in range(QB) for d in range(NY - 1)]):
        at(n, rows[b].start)
    for p in range(PHASES):
        at(SPOT[p, 0, 3], lambda p=p: edges_go(p))
    at(6, edges_come)
    for qb in range(QB):
        at(6 + qb, lambda qb=qb: window_score(qb))
    at(DONE[0], rows_come)
    bounds = [0, 2, 4, 6, 8, 10, 12, 14, 16]
    for n in range(8):
        at(DONE[0] + n, lambda n=n: lax.fori_loop(bounds[n], bounds[n + 1], score, 0))
    at(DONE[0] + 8, stats_go)
    for h in range(HEADS - 1):
        for i in range(QB):
            at(DONE[h + 1] + i, lambda h=h, i=i: weigh(h, i))
        at(DONE[h + 1] + QB, lambda h=h: window_weigh(h))
    at(DONE[2] + 5, stats_come)
    for i in range(QB):
        at(DONE[2] + 6 + i, lambda i=i: merge(0, i))
        at(DONE[3] + 1 + i, lambda i=i: merge(1, i))
    at(DONE[3] + 5, swaps_go)
    at(DONE[3] + 7, swaps_come, lambda: lax.fori_loop(0, TILES // 2, project_early, 0))
    at(DONE[3] + 8, lambda: lax.fori_loop(TILES // 2, TILES, project_early, 0))
    assert max(work) < RING

    for r in range(RING):
        for way in range(2):
            rings[way][r].wait_recv()
            for n in follow.get(r, ()):
                rings[way][n].start()
        for call in work.get(r, ()):
            call()

    last = HEADS - 1
    for i in range(QB):
        weigh(last, i)
    window_weigh(last)

    sends = []
    for i in range(QB):
        merge(last - 1, i)
        merge(last, i)
        swaps[1][i].start()

        def own(n, carry):
            cols = pl.ds(pl.multiple_of(n * TILE, TILE), TILE)
            total[i, :, cols] += jnp.dot(att[i, mine, late], w_own[late, cols], preferred_element_type=jnp.float32)
            return carry

        lax.fori_loop(0, TILES, own, 0)
        swaps[1][i].wait_recv()
        if 1 <= i < 3:
            sends[i - 1].wait_recv()
        if i == 3:
            sends[2].wait_recv()
            sends[3].wait_recv()

        def value_of(cols):
            return total[i, :, cols] + jnp.dot(
                att_other[i, :, late], w_other[late, cols], preferred_element_type=jnp.float32)

        def other(n, carry):
            cols = pl.ds(pl.multiple_of(n * TILE, TILE), TILE)
            value = value_of(cols)
            if i == 3:
                value += final[0, :, cols].astype(jnp.float32) + final[1, :, cols].astype(jnp.float32)
                out_ref[:, cols] = value.astype(jnp.bfloat16)
            else:
                sent[i, :, cols] = value.astype(jnp.bfloat16)
            return carry

        def other_relay(n, carry):
            cols = pl.ds(pl.multiple_of(n * TILE + (i - 1) * MIDDLE, TILE), TILE)
            near = pl.ds(pl.multiple_of(n * TILE, TILE), TILE)
            value = value_of(cols) + relay[i - 1, :, near].astype(jnp.float32)
            sent[i, :, cols] = value.astype(jnp.bfloat16)
            return carry

        if i == 1:
            lax.fori_loop(TILES // 2, TILES, other, 0)
            lax.fori_loop(0, TILES // 2, other_relay, 0)
        elif i == 2:
            lax.fori_loop(0, TILES // 2, other, 0)
            lax.fori_loop(0, TILES // 2, other_relay, 0)
        else:
            lax.fori_loop(0, TILES, other, 0)
        if i == 0:
            for s, peer in enumerate((right, left)):
                sends.append(remote(sent.at[0, :, pl.ds(s * MIDDLE, MIDDLE)], relay.at[s],
                                    x_send.at[s], x_recv.at[s], {"mp": peer}))
                sends[-1].start()
        elif i < 3:
            sends.append(remote(sent.at[i], final.at[i - 1], x_send.at[i + 1], x_recv.at[i + 1],
                                {"mp": right if i == 1 else left}))
            sends[-1].start()

    groups = edges + rings + swaps + [rows, numbers, stats, sends] + [c for h in range(HEADS) for c in parts[h]]
    for copies in groups:
        for copy in copies:
            copy.wait_send()


def shards(query_rows, key_rows, value_rows, out_weight, random_ids, global_ids):
    bf, f32 = jnp.bfloat16, jnp.float32
    dma = pltpu.SemaphoreType.DMA
    vmem = pltpu.VMEM
    ids = jnp.pad(random_ids, ((0, 8 - QB), (0, 128 - RAND)))
    anywhere = pl.BlockSpec(memory_space=pl.ANY)
    blocks = (QB, BLK, FEATS)
    return pl.pallas_call(
        kernel,
        name="attend_and_project",
        out_shape=jax.ShapeDtypeStruct((HALF, WIDTH), bf),
        in_specs=[anywhere] * 5 + [pl.BlockSpec(memory_space=pltpu.SMEM)],
        out_specs=pl.BlockSpec(memory_space=pltpu.VMEM),
        scratch_shapes=[
            vmem((NZ * QB, BLK, FEATS), bf),
            *[vmem((NZ * QB, HD, BLK), bf)] * HEADS,
            vmem((NY * QB, BLK, FEATS), bf),
            vmem((NY, 8, 128), jnp.int32),
            pltpu.SMEM((NY, 8, 128), jnp.int32),
            vmem((2, BLK, FEATS), bf),
            vmem((2 * HEADS, HD, BLK), bf),
            vmem(blocks, bf),
            vmem((QB, FEATS, BLK), f32),
            vmem((QB, 2 * HEADS, BLK), f32),
            vmem((QB, HEADS, 3 * BLK, BLK), bf),
            vmem((NY * QB, HEADS, CAND * BLK, BLK), bf),
            vmem((NY * QB, FEATS, BLK), bf),
            vmem((NY * QB, 2 * HEADS, BLK), f32),
            vmem((NY - 1, QB, FEATS, BLK), bf),
            vmem((NY - 1, QB, 2 * HEADS, BLK), f32),
            vmem((FEATS, WIDTH), bf),
            vmem((FEATS, WIDTH), bf),
            vmem((QB, BLK, FEATS), bf),
            vmem((QB, HALF, FEATS), bf),
            vmem((3, HALF, WIDTH), bf),
            vmem((2, HALF, WIDTH // 2), bf),
            vmem((2, HALF, WIDTH), bf),
            vmem((QB, HALF, WIDTH), f32),
            dma((2, RING)), dma((2, RING)), dma((NY - 1, QB)), dma((NY - 1, QB)), dma((NY - 1,)), dma((NY - 1,)),
            dma((PHASES, 2)), dma((PHASES, 2)), dma((2,)), dma((6,)),
            dma((HEADS, NY - 1, QB)), dma((HEADS, NY - 1, QB)), dma((NY - 1,)), dma((NY - 1,)),
            dma((2, QB)), dma((2, QB)), dma((4,)), dma((4,)),
        ],
        compiler_params=pltpu.CompilerParams(
            collective_id=0, has_side_effects=True, vmem_limit_bytes=56 * MIB
        ),
        cost_estimate=pl.CostEstimate(flops=4 * 10**9, bytes_accessed=24 * MIB, transcendentals=0),
    )(
        query_rows.reshape(blocks), key_rows.reshape(blocks), value_rows.reshape(blocks),
        out_weight, ids, global_ids,
    )


def solution(mesh):
    return jax.shard_map(
        shards,
        mesh=mesh,
        in_specs=(
            P("ctx", "mp"),
            P("ctx", "mp"),
            P("ctx", "mp"),
            P("mp", None),
            P("ctx", None),
            P(),
        ),
        out_specs=P(("ctx", "mp"), None),
        check_vma=False,
    )
```

time: 152 us -> 141 us (0.928)
  Pallas kernels: 148 us -> 138 us
    pallas_call x1, Pallas kernels: 148 us -> 138 us  [shards(): pl.pallas_call(kernel, name='attend_and_project', out_shape=jax.ShapeDtyp...]
where the time goes in v3:
time: 141 us
  Pallas kernels  138 us (98%)
  local copies, waits for them, and re-layouts  3.15 us (2%)
    pallas_call x1, Pallas kernels, shards(): pl.pallas_call(kernel, name='attend_and_project', out_shape=jax.ShapeDtyp...  138 us

profile of v3, /device:TPU:1, one launch (start us, length us, event | category | flops | bytes accessed | tf_op | source)
XLA Modules:
  0.0 140.8 jit_solution(4534737212272472866)
XLA Ops:
  0.0 1.3 pad.4.ids_ref
  1.3 137.6 %attend_and_project.1 = bf16[64,4096]{1,0:T(8,128)(2,1)} custom-call(bf16[4,128,512]{2,1,0:T(8,128)(2,1)} %bitcast.3, bf16[4,128,512]{2,1,0:T(8,128)(2,1)} %bitcast.4, bf16[4,128,512]{2,1,0:T(8,128)(2,1)} %bitcast.5, bf16[512,4096]{1,0:T(8,128)(2,1)} %w_ref.1, s32[8,128]{1,0:T(8,128)} %pad.4.ids_ref, s32[2]{0:T(128)} %glob_ref.1), custom_call_target="tpu_custom_call" | custom-call | flops 4000000000 | bytes 25165824 | tf_op jit(solution)/shard_map/attend_and_project/pallas_call | solution.py:414
  138.9 1.9 %copy.8 = bf16[64,4096]{1,0:T(8,128)(2,1)} copy(bf16[64,4096]{1,0:T(8,128)(2,1)} %attend_and_project.1) | data formatting | bytes 1048576

commit v4 on v3

v4 whole, which is shorter than its diff:
```python
import math

import jax
import jax.numpy as jnp
from jax import lax
from jax.experimental import pallas as pl
from jax.experimental.pallas import tpu as pltpu
from jax.sharding import PartitionSpec as P

HD = 128
BLK = 128
RAND = 3
GLOB = 2
CAND = GLOB + RAND
NZ = 8
NY = 4
NX = 4
HEADS = 4
QB = 4
FEATS = HEADS * HD
WIDTH = 4096
HALF = BLK // 2
TILE = 512
SCALE = 1.0 / math.sqrt(HD)
LOW = -1e30
MESH = pl.DeviceIdType.MESH
NT = (((1,), (1,)), ((), ()))
PHASES = 2 + HEADS
LATE = HEADS - 1
MAIN = LATE * HD
KINDS = ((0, 0), (1, 0), (1, 1), (1, 2), (0, 1), (1, 3))
V_PHASE = (1, 2, 3, 5)
CUTS = 4
CUT = HD // CUTS
TILES = WIDTH // TILE
MIDDLE = WIDTH // 2
MIB = 1024 * 1024


def ring_order():
    order = [(0, 0, j) for j in range(4)]
    for p in range(PHASES):
        ahead = [(p + 1, 0, j) for j in range(4)] if p + 1 < PHASES else []
        order += [(p, 1, j) for j in range(4)] + ahead[:2]
        order += [(p, 2, j) for j in range(4)] + ahead[2:]
        order += [(p, 3, j) for j in range(2)]
    return order


ORDER = ring_order()
RING = len(ORDER)
SPOT = {item: n for n, item in enumerate(ORDER)}
DONE = [SPOT[p, 3, 1] for p in range(PHASES)]


def followers():
    follow, last = {}, -1
    for n, (p, back, j) in enumerate(ORDER):
        if back > 0:
            last = max(last, SPOT[p, back - 1, j])
        follow.setdefault(last, []).append(n)
    return follow


def kernel(
    q_ref, k_ref, v_ref, w_ref, ids_ref, glob_ref, out_ref,
    k_main, k_late, v_col0, v_col1, v_col2, v_col3, q_row, id_row, id_s, k_edge, k_edge_late, v_edge, v_own, acc, w_stat, w_probs,
    probs, part, p_stat, p_late, got, got_stat, got_late, w_own, w_other, w_far,
    att, att_other, att_late, come_late, sent, relay, final, total,
    ring_send, ring_recv, row_send, row_recv, id_send, id_recv, edge_send, edge_recv, w_sem, local_sem,
    part_send, part_recv, stat_send, stat_recv, att_send, att_recv, x_send, x_recv,
    far_send, far_recv, pass_send, pass_recv, late_send, late_recv,
):
    me, mp = lax.axis_index("ctx"), lax.axis_index("mp")
    z, y, x, core = me // NY, me % NY, mp // 2, mp % 2
    count = NZ * NY
    sibling = mp + 1 - 2 * core
    up, down = (z + 1) % NZ, (z + NZ - 1) % NZ
    right, left = ((x + 1) % NX) * 2 + core, ((x + NX - 1) % NX) * 2 + core
    order = [(x + d) % NX for d in (2, 1, 3, 0)]
    v_cols = (v_col0, v_col1, v_col2, v_col3)
    k_cols, k_edges = (k_main, k_late), (k_edge, k_edge_late)
    main, late = pl.ds(0, MAIN), pl.ds(MAIN, HD)

    local = [
        pltpu.make_async_copy(v_ref, v_own, local_sem.at[0]),
        pltpu.make_async_copy(q_ref, q_row.at[pl.ds(y * QB, QB)], local_sem.at[1]),
        pltpu.make_async_copy(k_ref.at[:, :, main], k_main.at[pl.ds(z * QB, QB)], local_sem.at[2]),
        pltpu.make_async_copy(k_ref.at[:, :, late], k_late.at[pl.ds(z * QB, QB)], local_sem.at[6]),
        pltpu.make_async_copy(ids_ref, id_row.at[y], local_sem.at[3]),
        pltpu.make_async_copy(w_ref, w_own, local_sem.at[4]),
    ]
    for copy in local:
        copy.start()

    barrier = pltpu.get_barrier_semaphore()
    peers = [{"ctx": up * NY + y}, {"ctx": down * NY + y}]
    peers += [{"ctx": z * NY + (y + d) % NY} for d in range(1, NY)]
    peers += [{"mp": sibling}] + [{"mp": ((x + d) % NX) * 2 + c} for d in range(1, NX) for c in range(2)]
    for peer in peers:
        pl.semaphore_signal(barrier, inc=1, device_id=peer, device_id_type=MESH)
    pl.semaphore_wait(barrier, len(peers))

    def remote(src, dst, send, recv, peer):
        return pltpu.make_async_remote_copy(
            src_ref=src, dst_ref=dst, send_sem=send, recv_sem=recv, device_id=peer, device_id_type=MESH
        )

    def ring(way, n):
        p, back, j = ORDER[n]
        sign = 1 if way == 0 else -1
        peer = {"ctx": (up if way == 0 else down) * NY + y}
        sems = (ring_send.at[way, n], ring_recv.at[way, n])
        piece = (j + 2 * way) % 4
        block = ((z + NZ - sign * back) % NZ) * QB + piece
        kind, index = KINDS[p]
        ref = (k_cols, v_cols)[kind][index]
        src = ref.at[block]
        if kind == 0 and back == 0:
            src = k_ref.at[piece, :, (main, late)[index]]
        return remote(src, ref.at[block], *sems, peer)

    rings = [[ring(way, n) for n in range(RING)] for way in range(2)]
    follow = followers()
    for n in follow[-1]:
        rings[0][n].start()
        rings[1][n].start()

    above = jnp.where(y < NY - 1, z, down) * QB + QB - 1
    below = jnp.where(y > 0, z, up) * QB
    next_y, last_y = {"ctx": z * NY + (y + 1) % NY}, {"ctx": z * NY + (y + NY - 1) % NY}
    edges = []
    for p, (kind, index) in enumerate(KINDS):
        source = (k_cols, v_cols)[kind][index]
        target = v_edge if kind else k_edges[index]
        spots = (2 * index, 2 * index + 1) if kind else (0, 1)
        edges.append([
            remote(source.at[above], target.at[spots[0]], edge_send.at[p, 0], edge_recv.at[p, 0], next_y),
            remote(source.at[below], target.at[spots[1]], edge_send.at[p, 1], edge_recv.at[p, 1], last_y),
        ])
    numbers, rows = [], []
    for d in range(1, NY):
        peer = {"ctx": z * NY + (y + d) % NY}
        numbers.append(remote(ids_ref, id_row.at[y], id_send.at[d - 1], id_recv.at[d - 1], peer))
        for b in range(QB):
            rows.append(remote(q_ref.at[b], q_row.at[y * QB + b], row_send.at[d - 1, b], row_recv.at[d - 1, b], peer))
    for copy in numbers:
        copy.start()
    weight = remote(w_ref, w_other, w_sem.at[0], w_sem.at[1], {"mp": sibling})
    weight.start()

    local[0].wait()

    def turn(b, carry):
        for h in range(HEADS):
            v_cols[h][z * QB + b] = v_own[b, :, pl.ds(h * HD, HD)].T
        return carry

    lax.fori_loop(0, QB, turn, 0)
    for copy in local[1:]:
        copy.wait()

    def key_part(h):
        return (k_late, k_edge_late, pl.ds(0, HD)) if h == LATE else (k_main, k_edge, pl.ds(h * HD, HD))

    def window_score(qb, heads):
        row = lax.broadcasted_iota(jnp.int32, (3 * BLK, 1), 0)
        first = jnp.where(me + qb == 0, BLK, 0)
        last = jnp.where(me * QB + qb == count * QB - 1, 2 * BLK, 3 * BLK)
        live = (row >= first) & (row < last)
        for h in heads:
            k_col, edge, cols = key_part(h)
            keys = [edge[0, :, cols] if qb == 0 else k_col[z * QB + qb - 1, :, cols]]
            keys.append(k_col[z * QB + qb, :, cols])
            keys.append(edge[1, :, cols] if qb == QB - 1 else k_col[z * QB + qb + 1, :, cols])
            s = lax.dot_general(jnp.concatenate(keys, axis=0), q_row[y * QB + qb, :, pl.ds(h * HD, HD)], NT,
                                preferred_element_type=jnp.float32) * SCALE
            s = jnp.where(live, s, LOW)
            top = jnp.max(s, axis=0, keepdims=True)
            p = jnp.exp(s - top).astype(jnp.bfloat16)
            w_stat[qb, pl.ds(h, 1), :] = top
            w_stat[qb, pl.ds(HEADS + h, 1), :] = jnp.sum(p.astype(jnp.float32), axis=0, keepdims=True)
            w_probs[qb, h] = p

    def window_weigh(h):
        for copy in edges[V_PHASE[h]]:
            copy.wait_recv()
        for qb in range(QB):
            values = [v_edge[2 * h] if qb == 0 else v_cols[h][z * QB + qb - 1]]
            values.append(v_cols[h][z * QB + qb])
            values.append(v_edge[2 * h + 1] if qb == QB - 1 else v_cols[h][z * QB + qb + 1])
            acc[qb, pl.ds(h * HD, HD), :] = jnp.dot(
                jnp.concatenate(values, axis=1), w_probs[qb, h], preferred_element_type=jnp.float32)

    def candidates(t):
        blocks = [glob_ref[j] for j in range(GLOB)]
        blocks += [id_s[lax.div(t, QB), lax.rem(t, QB), j] for j in range(RAND)]
        spots = [lax.div(block, NY * QB) * QB + lax.rem(block, QB) for block in blocks]
        return blocks, spots

    def stat_lines(h):
        return (0, 1) if h == LATE else (h, HEADS + h)

    def score(t, heads):
        blocks, spots = candidates(t)
        bias = [jnp.where(lax.rem(lax.div(block, QB), NY) == y, 0.0, LOW) for block in blocks]
        for h in heads:
            k_col, _, cols = key_part(h)
            stat = p_late if h == LATE else p_stat
            top_line, sum_line = stat_lines(h)
            keys = jnp.concatenate([k_col[spot, :, cols] for spot in spots], axis=0)
            s = lax.dot_general(keys, q_row[t, :, pl.ds(h * HD, HD)], NT, preferred_element_type=jnp.float32)
            s = jnp.concatenate([s[j * BLK:(j + 1) * BLK] * SCALE + bias[j] for j in range(CAND)], axis=0)
            top = jnp.max(s, axis=0, keepdims=True)
            p = jnp.exp(s - top).astype(jnp.bfloat16)
            stat[t, pl.ds(top_line, 1), :] = top
            stat[t, pl.ds(sum_line, 1), :] = jnp.sum(p.astype(jnp.float32), axis=0, keepdims=True)
            probs[t, h] = p

    def score_main(t, carry):
        score(t, range(LATE))
        return carry

    def score_late(t, carry):
        score(t, (LATE,))
        return carry

    stats = [[], []]
    for d in range(1, NY):
        to = (y + d) % NY
        for n, (stat, got_one) in enumerate(((p_stat, got_stat), (p_late, got_late))):
            stats[n].append(remote(stat.at[pl.ds(to * QB, QB)], got_one.at[d - 1], stat_send.at[n, d - 1],
                                   stat_recv.at[n, d - 1], {"ctx": z * NY + to}))

    def returns(h, i):
        span = pl.ds(h * HD, HD)
        copies = []
        for d in (2, 1, 3):
            to = (y + d) % NY
            copies.append(remote(part.at[to * QB + order[i], span], got.at[d - 1, order[i], span],
                                 part_send.at[h, d - 1, i], part_recv.at[h, d - 1, i], {"ctx": z * NY + to}))
        return copies

    parts = [[returns(h, i) for i in range(QB)] for h in range(HEADS)]

    def weigh(h, i):
        def one(to, carry):
            t = to * QB + order[i]
            spots = candidates(t)[1]
            values = jnp.concatenate([v_cols[h][spot] for spot in spots], axis=1)
            out = jnp.dot(values, probs[t, h], preferred_element_type=jnp.float32)
            out = out / (p_late if h == LATE else p_stat)[t, pl.ds(stat_lines(h)[1], 1), :]
            part[t, pl.ds(h * HD, HD), :] = out.astype(jnp.bfloat16)
            return carry

        lax.fori_loop(0, NY, one, 0)
        for copy in parts[h][i]:
            copy.start()

    def merge(h, i):
        for copy in parts[h][i]:
            copy.wait_recv()
        qb = order[i]
        cols = pl.ds(h * HD, HD)
        line, low_line = pl.ds(h, 1), pl.ds(HEADS + h, 1)
        one, other = (p_late, got_late) if h == LATE else (p_stat, got_stat)
        there, low_there = [pl.ds(n, 1) for n in stat_lines(h)]
        tops = [w_stat[qb, line, :], one[y * QB + qb, there, :]]
        tops += [other[s, qb, there, :] for s in range(NY - 1)]
        sums = [w_stat[qb, low_line, :], one[y * QB + qb, low_there, :]]
        sums += [other[s, qb, low_there, :] for s in range(NY - 1)]
        best = tops[0]
        for top in tops[1:]:
            best = jnp.maximum(best, top)
        scales = [jnp.exp(top - best) for top in tops]
        weights = [scale * total_of for scale, total_of in zip(scales, sums)]
        low = weights[0] + weights[1] + weights[2] + weights[3] + weights[4]
        value = acc[qb, cols, :] * (scales[0] / low)
        value += part[y * QB + qb, cols, :].astype(jnp.float32) * (weights[1] / low)
        for s in range(NY - 1):
            value += got[s, qb, cols, :].astype(jnp.float32) * (weights[s + 2] / low)
        if h == LATE:
            att_late[i] = value.T.astype(jnp.bfloat16)
        else:
            att[i, :, cols] = value.T.astype(jnp.bfloat16)

    mine = pl.ds(pl.multiple_of(core * HALF, HALF), HALF)
    theirs = pl.ds(pl.multiple_of((1 - core) * HALF, HALF), HALF)
    swaps = [remote(att.at[i, theirs], att_other.at[i], att_send.at[i], att_recv.at[i], {"mp": sibling})
             for i in range(QB)]

    def project(n, carry):
        cols = pl.ds(pl.multiple_of(n * TILE, TILE), TILE)
        own = jnp.concatenate([att[i, mine, :] for i in range(QB)], axis=0)
        other = jnp.concatenate([att_other[i] for i in range(QB)], axis=0)
        value = jnp.dot(own, w_own[main, cols], preferred_element_type=jnp.float32)
        value += jnp.dot(other, w_other[main, cols], preferred_element_type=jnp.float32)
        for i in range(QB):
            total[i, :, cols] = value[i * HALF:(i + 1) * HALF]
        return carry

    far = [[], []]
    for way, peer in enumerate(({"mp": right}, {"mp": left})):
        from_d, to_d = (2, 0)[way], (2, 0)[way]
        for c in range(CUTS):
            rows_of = pl.ds(pl.multiple_of(core * HD + c * CUT, CUT), CUT)
            far[way].append(remote(w_ref.at[pl.ds(MAIN + c * CUT, CUT)], w_far.at[to_d, rows_of],
                                   far_send.at[way, c], far_recv.at[way, c], peer))
        for n in range(CUTS // 2):
            c = n + way * (CUTS // 2)
            rows_of = pl.ds(pl.multiple_of(core * HD + c * CUT, CUT), CUT)
            far[way].append(remote(w_far.at[from_d, rows_of], w_far.at[1, rows_of],
                                   far_send.at[way, CUTS + n], far_recv.at[way, CUTS + n], peer))
    own_half = pl.ds(pl.multiple_of(core * HD, HD), HD)
    passed = [remote(w_far.at[d, own_half], w_far.at[d, own_half], pass_send.at[d], pass_recv.at[d], {"mp": sibling})
              for d in range(NX - 1)]

    lates = []
    for i, qb in enumerate(order):
        lates.append([])
        for c in range(2):
            if i < QB - 1:
                lates[i].append(remote(att_late.at[i, pl.ds(c * HALF, HALF)], come_late.at[mp],
                                       late_send.at[i, c], late_recv.at[i, core], {"mp": qb * 2 + c}))
    lates[QB - 1].append(remote(att_late.at[QB - 1, theirs], come_late.at[mp],
                                late_send.at[QB - 1, 0], late_recv.at[QB - 1, core], {"mp": sibling}))

    sends = [remote(sent.at[0, :, pl.ds(s * MIDDLE, MIDDLE)], relay.at[s], x_send.at[s], x_recv.at[s], {"mp": peer})
             for s, peer in enumerate((right, left))]
    sends += [remote(sent.at[i], final.at[i - 1], x_send.at[i + 1], x_recv.at[i + 1], {"mp": peer})
              for i, peer in ((1, right), (2, left))]

    def send_first():
        sent[0] = total[0].astype(jnp.bfloat16)
        sends[0].start()
        sends[1].start()

    def send_relayed(i):
        sends[i - 1].wait_recv()
        here, there = pl.ds((i - 1) * MIDDLE, MIDDLE), pl.ds((2 - i) * MIDDLE, MIDDLE)
        sent[i, :, here] = (total[i, :, here] + relay[i - 1].astype(jnp.float32)).astype(jnp.bfloat16)
        sent[i, :, there] = total[i, :, there].astype(jnp.bfloat16)
        sends[i + 1].start()

    work = {}

    def at(r, *calls):
        work.setdefault(r, []).extend(calls)

    def edges_go(p):
        for copy in edges[p]:
            copy.start()

    def edges_come():
        for copy in edges[0]:
            copy.wait_recv()

    def rows_come():
        for copy in rows + numbers:
            copy.wait_recv()
        to_scalar = pltpu.make_async_copy(id_row, id_s, local_sem.at[5])
        to_scalar.start()
        to_scalar.wait()

    def stats_go(n):
        for copy in stats[n]:
            copy.start()

    def stats_come(n):
        for copy in stats[n]:
            copy.wait_recv()

    def swaps_go():
        for copy in swaps:
            copy.start()

    def swaps_come():
        for copy in swaps:
            copy.wait_recv()
        weight.wait()

    def far_go(n):
        for way in range(2):
            if n >= CUTS:
                far[way][n - CUTS + way * (CUTS // 2)].wait_recv()
            far[way][n].start()

    def pass_near():
        for way, d in ((0, 2), (1, 0)):
            for n in range(CUTS // 2):
                far[way][n + (1 - way) * (CUTS // 2)].wait_recv()
            passed[d].start()

    def pass_far():
        for way in range(2):
            for n in range(CUTS, CUTS + CUTS // 2):
                far[way][n].wait_recv()
        passed[1].start()

    def late_scores(n):
        if n == 0:
            for copy in edges[4]:
                copy.wait_recv()
            for qb in range(QB):
                window_score(qb, (LATE,))
        lax.fori_loop(n * 4, n * 4 + 4, score_late, 0)

    for n, b in enumerate([d * QB + b for b in range(QB) for d in range(NY - 1)]):
        at(n, rows[b].start)
    for p in range(PHASES):
        at(SPOT[p, 0, 3], lambda p=p: edges_go(p))
    at(6, edges_come)
    for qb in range(QB):
        at(6 + qb, lambda qb=qb: window_score(qb, range(LATE)))
    at(DONE[0], rows_come)
    bounds = [0, 2, 4, 6, 8, 10, 12, 14, 16]
    for n in range(8):
        at(DONE[0] + n, lambda n=n: lax.fori_loop(bounds[n], bounds[n + 1], score_main, 0))
    at(DONE[0] + 8, lambda: stats_go(0))
    for n, r in enumerate((1, 4, 7, 10, 13, DONE[0] + 2)):
        at(r, lambda n=n: far_go(n))
    at(DONE[0] + 8, pass_near)
    at(DONE[1] + 5, pass_far)
    for h in range(LATE):
        for i in range(QB):
            at(DONE[h + 1] + i, lambda h=h, i=i: weigh(h, i))
        at(DONE[h + 1] + QB, lambda h=h: window_weigh(h))
    at(DONE[2] + 5, lambda: stats_come(0))
    for i in range(QB):
        at(DONE[2] + 6 + i, lambda i=i: merge(0, i))
        at(DONE[3] + 5 + i, lambda i=i: merge(1, i))
        at(DONE[4], lambda i=i: merge(2, i))
    at(DONE[4], swaps_go)
    at(DONE[4] + 1, lambda: late_scores(0))
    at(DONE[4] + 2, lambda: late_scores(1))
    at(DONE[4] + 3, swaps_come, lambda: lax.fori_loop(0, TILES // 2, project, 0))
    at(DONE[4] + 4, lambda: lax.fori_loop(TILES // 2, TILES, project, 0), send_first)
    at(DONE[4] + 5, lambda: late_scores(2))
    at(DONE[4] + 6, lambda: late_scores(3), lambda: stats_go(1))
    assert max(work) < RING

    for r in range(RING):
        for way in range(2):
            rings[way][r].wait_recv()
            for n in follow.get(r, ()):
                rings[way][n].start()
        for call in work.get(r, ()):
            call()

    for i in range(QB):
        weigh(LATE, i)
    window_weigh(LATE)
    send_relayed(1)
    send_relayed(2)
    for copy in stats[1]:
        copy.wait_recv()
    for i in range(QB):
        merge(LATE, i)
        for copy in lates[i]:
            copy.start()
    come_late[mp] = att_late[QB - 1, mine, :]
    for copy in passed:
        copy.wait_recv()
    for i in range(QB - 1):
        for c in range(2):
            remote(att_late.at[i, pl.ds(0, HALF)], come_late.at[mp], late_send.at[i, c], late_recv.at[i, c],
                   {"mp": sibling}).wait_recv()
    remote(att_late.at[QB - 1, theirs], come_late.at[mp], late_send.at[QB - 1, 0], late_recv.at[QB - 1, 1 - core],
           {"mp": sibling}).wait_recv()
    sends[2].wait_recv()
    sends[3].wait_recv()

    def finish(n, carry):
        cols = pl.ds(pl.multiple_of(n * TILE, TILE), TILE)
        value = total[QB - 1, :, cols] + jnp.dot(come_late[mp], w_own[late, cols], preferred_element_type=jnp.float32)
        value += jnp.dot(come_late[sibling], w_other[late, cols], preferred_element_type=jnp.float32)
        for d in range(1, NX):
            chip = ((x + d) % NX) * 2
            pair = jnp.concatenate([come_late[chip], come_late[chip + 1]], axis=1)
            value += jnp.dot(pair, w_far[d - 1, :, cols], preferred_element_type=jnp.float32)
        value += final[0, :, cols].astype(jnp.float32) + final[1, :, cols].astype(jnp.float32)
        out_ref[:, cols] = value.astype(jnp.bfloat16)
        return carry

    lax.fori_loop(0, TILES, finish, 0)

    groups = edges + rings + far + lates + stats + [rows, numbers, swaps, sends, passed]
    groups += [c for h in range(HEADS) for c in parts[h]]
    for copies in groups:
        for copy in copies:
            copy.wait_send()


def shards(query_rows, key_rows, value_rows, out_weight, random_ids, global_ids):
    bf, f32 = jnp.bfloat16, jnp.float32
    dma = pltpu.SemaphoreType.DMA
    vmem = pltpu.VMEM
    ids = jnp.pad(random_ids, ((0, 8 - QB), (0, 128 - RAND)))
    anywhere = pl.BlockSpec(memory_space=pl.ANY)
    blocks = (QB, BLK, FEATS)
    return pl.pallas_call(
        kernel,
        name="attend_and_project",
        out_shape=jax.ShapeDtypeStruct((HALF, WIDTH), bf),
        in_specs=[anywhere] * 5 + [pl.BlockSpec(memory_space=pltpu.SMEM)],
        out_specs=pl.BlockSpec(memory_space=pltpu.VMEM),
        scratch_shapes=[
            vmem((NZ * QB, BLK, MAIN), bf),
            vmem((NZ * QB, BLK, HD), bf),
            *[vmem((NZ * QB, HD, BLK), bf)] * HEADS,
            vmem((NY * QB, BLK, FEATS), bf),
            vmem((NY, 8, 128), jnp.int32),
            pltpu.SMEM((NY, 8, 128), jnp.int32),
            vmem((2, BLK, MAIN), bf),
            vmem((2, BLK, HD), bf),
            vmem((2 * HEADS, HD, BLK), bf),
            vmem(blocks, bf),
            vmem((QB, FEATS, BLK), f32),
            vmem((QB, 2 * HEADS, BLK), f32),
            vmem((QB, HEADS, 3 * BLK, BLK), bf),
            vmem((NY * QB, HEADS, CAND * BLK, BLK), bf),
            vmem((NY * QB, FEATS, BLK), bf),
            vmem((NY * QB, 2 * HEADS, BLK), f32),
            vmem((NY * QB, 2 * HEADS, BLK), f32),
            vmem((NY - 1, QB, FEATS, BLK), bf),
            vmem((NY - 1, QB, 2 * HEADS, BLK), f32),
            vmem((NY - 1, QB, 2 * HEADS, BLK), f32),
            vmem((FEATS, WIDTH), bf),
            vmem((FEATS, WIDTH), bf),
            vmem((NX - 1, 2 * HD, WIDTH), bf),
            vmem((QB, BLK, MAIN), bf),
            vmem((QB, HALF, MAIN), bf),
            vmem((QB, BLK, HD), bf),
            vmem((2 * NX, HALF, HD), bf),
            vmem((3, HALF, WIDTH), bf),
            vmem((2, HALF, WIDTH // 2), bf),
            vmem((2, HALF, WIDTH), bf),
            vmem((QB, HALF, WIDTH), f32),
            dma((2, RING)), dma((2, RING)), dma((NY - 1, QB)), dma((NY - 1, QB)), dma((NY - 1,)), dma((NY - 1,)),
            dma((PHASES, 2)), dma((PHASES, 2)), dma((2,)), dma((7,)),
            dma((HEADS, NY - 1, QB)), dma((HEADS, NY - 1, QB)), dma((2, NY - 1)), dma((2, NY - 1)),
            dma((QB,)), dma((QB,)), dma((4,)), dma((4,)),
            dma((2, 6)), dma((2, 6)), dma((NX - 1,)), dma((NX - 1,)), dma((QB, 2)), dma((QB, 2)),
        ],
        compiler_params=pltpu.CompilerParams(
            collective_id=0, has_side_effects=True, vmem_limit_bytes=60 * MIB
        ),
        cost_estimate=pl.CostEstimate(flops=4 * 10**9, bytes_accessed=24 * MIB, transcendentals=0),
    )(
        query_rows.reshape(blocks), key_rows.reshape(blocks), value_rows.reshape(blocks),
        out_weight, ids, global_ids,
    )


def solution(mesh):
    return jax.shard_map(
        shards,
        mesh=mesh,
        in_specs=(
            P("ctx", "mp"),
            P("ctx", "mp"),
            P("ctx", "mp"),
            P("mp", None),
            P("ctx", None),
            P(),
        ),
        out_specs=P(("ctx", "mp"), None),
        check_vma=False,
    )
```

time: 141 us -> 129 us (0.915)
  Pallas kernels: 138 us -> 125 us
    pallas_call x1, Pallas kernels: 138 us -> 125 us  [shards(): pl.pallas_call(kernel, name='attend_and_project', out_shape=jax.ShapeDtyp...]
where the time goes in v4:
time: 129 us
  Pallas kernels  125 us (97%)
  local copies, waits for them, and re-layouts  3.15 us (2%)
    pallas_call x1, Pallas kernels, shards(): pl.pallas_call(kernel, name='attend_and_project', out_shape=jax.ShapeDtyp...  125 us

profile of v4, /device:TPU:1, one launch (start us, length us, event | category | flops | bytes accessed | tf_op | source)
XLA Modules:
  0.0 128.5 jit_solution(4730363467712442519)
XLA Ops:
  0.0 1.3 pad.4.ids_ref
  1.3 125.4 %attend_and_project.1 = bf16[64,4096]{1,0:T(8,128)(2,1)} custom-call(bf16[4,128,512]{2,1,0:T(8,128)(2,1)} %bitcast.3, bf16[4,128,512]{2,1,0:T(8,128)(2,1)} %bitcast.4, bf16[4,128,512]{2,1,0:T(8,128)(2,1)} %bitcast.5, bf16[512,4096]{1,0:T(8,128)(2,1)} %w_ref.1, s32[8,128]{1,0:T(8,128)} %pad.4.ids_ref, s32[2]{0:T(128)} %glob_ref.1), custom_call_target="tpu_custom_call" | custom-call | flops 4000000000 | bytes 25165824 | tf_op jit(solution)/shard_map/attend_and_project/pallas_call | solution.py:501
  126.6 1.9 %copy.8 = bf16[64,4096]{1,0:T(8,128)(2,1)} copy(bf16[64,4096]{1,0:T(8,128)(2,1)} %attend_and_project.1) | data formatting | bytes 1048576

commit v5 on v4

v5 whole, which is shorter than its diff:
```python
import math

import jax
import jax.numpy as jnp
from jax import lax
from jax.experimental import pallas as pl
from jax.experimental.pallas import tpu as pltpu
from jax.sharding import PartitionSpec as P

HD = 128
BLK = 128
RAND = 3
GLOB = 2
CAND = GLOB + RAND
NZ = 8
NY = 4
NX = 4
HEADS = 4
QB = 4
FEATS = HEADS * HD
WIDTH = 4096
HALF = BLK // 2
TILE = 512
SCALE = 1.0 / math.sqrt(HD)
LOW = -1e30
MESH = pl.DeviceIdType.MESH
NT = (((1,), (1,)), ((), ()))
PHASES = 2 * HEADS
LATE = HEADS - 1
MAIN = LATE * HD
CUTS = 4
CUT = HD // CUTS
TILES = WIDTH // TILE
MIDDLE = WIDTH // 2
MIB = 1024 * 1024


def ring_order():
    order = [(0, 0), (2, 0), (0, 1), (1, 0), (0, 2), (1, 1), (0, 3), (1, 2), (2, 1), (1, 3)]
    for p in range(2, PHASES - 1):
        order += [(p + 1, 0), (p, 2), (p + 1, 1), (p, 3)]
    order += [(PHASES - 1, 2), (PHASES - 1, 3)]
    return [(p, back, j) for p, back in order for j in range(1 if back == 3 else 2)]


ORDER = ring_order()
RING = len(ORDER)
SPOT = {item: n for n, item in enumerate(ORDER)}
DONE = [SPOT[p, 3, 0] for p in range(PHASES)]


def followers():
    follow, last = {}, -1
    for n, (p, back, j) in enumerate(ORDER):
        if back > 0:
            last = max(last, SPOT[p, back - 1, j])
        follow.setdefault(last, []).append(n)
    return follow


def kernel(
    q_ref, k_ref, v_ref, w_ref, ids_ref, glob_ref, out_ref,
    k_col0, k_col1, k_col2, k_col3, v_col0, v_col1, v_col2, v_col3, q_row0, q_row1, q_row2, q_row3,
    id_row, id_s, k_edge, v_edge, v_own, acc, w_stat, w_probs,
    probs, part, p_stat, got, got_stat, w_own, w_other, w_far,
    att, att_other, att_late, come_late, sent, relay, final, total,
    ring_send, ring_recv, row_send, row_recv, id_send, id_recv, edge_send, edge_recv, w_sem, local_sem,
    part_send, part_recv, stat_send, stat_recv, att_send, att_recv, x_send, x_recv,
    far_send, far_recv, pass_send, pass_recv, late_send, late_recv,
):
    me, mp = lax.axis_index("ctx"), lax.axis_index("mp")
    z, y, x, core = me // NY, me % NY, mp // 2, mp % 2
    count = NZ * NY
    sibling = mp + 1 - 2 * core
    up, down = (z + 1) % NZ, (z + NZ - 1) % NZ
    right, left = ((x + 1) % NX) * 2 + core, ((x + NX - 1) % NX) * 2 + core
    order = [(x + d) % NX for d in (2, 1, 3, 0)]
    v_cols = (v_col0, v_col1, v_col2, v_col3)
    k_cols = (k_col0, k_col1, k_col2, k_col3)
    q_rows = (q_row0, q_row1, q_row2, q_row3)
    main, late = pl.ds(0, MAIN), pl.ds(MAIN, HD)

    def head(h):
        return pl.ds(h * HD, HD)

    own_keys, own_rows = pl.ds(z * QB, QB), pl.ds(y * QB, QB)
    local = [
        pltpu.make_async_copy(v_ref, v_own, local_sem.at[0]),
        pltpu.make_async_copy(ids_ref, id_row.at[y], local_sem.at[1]),
        pltpu.make_async_copy(w_ref, w_own, local_sem.at[2]),
    ]
    k_local = [pltpu.make_async_copy(k_ref.at[:, :, head(h)], k_cols[h].at[own_keys], local_sem.at[4 + h])
               for h in range(HEADS)]
    q_local = [pltpu.make_async_copy(q_ref.at[:, :, head(h)], q_rows[h].at[own_rows], local_sem.at[8 + h])
               for h in range(HEADS)]
    for k_copy, q_copy in zip(k_local, q_local):
        local += [k_copy, q_copy]
    for copy in local:
        copy.start()

    barrier = pltpu.get_barrier_semaphore()
    peers = [{"ctx": up * NY + y}, {"ctx": down * NY + y}]
    peers += [{"ctx": z * NY + (y + d) % NY} for d in range(1, NY)]
    peers += [{"mp": sibling}] + [{"mp": ((x + d) % NX) * 2 + c} for d in range(1, NX) for c in range(2)]
    for peer in peers:
        pl.semaphore_signal(barrier, inc=1, device_id=peer, device_id_type=MESH)
    pl.semaphore_wait(barrier, len(peers))

    def remote(src, dst, send, recv, peer):
        return pltpu.make_async_remote_copy(
            src_ref=src, dst_ref=dst, send_sem=send, recv_sem=recv, device_id=peer, device_id_type=MESH
        )

    def ring(way, n):
        p, back, j = ORDER[n]
        sign = 1 if way == 0 else -1
        peer = {"ctx": (up if way == 0 else down) * NY + y}
        sems = (ring_send.at[way, n], ring_recv.at[way, n])
        piece = 2 * ((j + way) % 2)
        span = pl.ds(((z + NZ - sign * back) % NZ) * QB + piece, 2)
        if p % 2:
            ref = v_cols[p // 2]
            return remote(ref.at[span], ref.at[span], *sems, peer)
        ref = k_cols[p // 2]
        src = k_ref.at[pl.ds(piece, 2), :, head(p // 2)] if back == 0 else ref.at[span]
        return remote(src, ref.at[span], *sems, peer)

    rings = [[ring(way, n) for n in range(RING)] for way in range(2)]
    follow = followers()
    for n in follow[-1]:
        rings[0][n].start()
        rings[1][n].start()

    above = jnp.where(y < NY - 1, z, down) * QB + QB - 1
    below = jnp.where(y > 0, z, up) * QB
    next_y, last_y = {"ctx": z * NY + (y + 1) % NY}, {"ctx": z * NY + (y + NY - 1) % NY}
    edges = []
    for p in range(PHASES):
        source, target = (v_cols[p // 2], v_edge) if p % 2 else (k_cols[p // 2], k_edge)
        spots = (p // 2 * 2, p // 2 * 2 + 1)
        edges.append([
            remote(source.at[above], target.at[spots[0]], edge_send.at[p, 0], edge_recv.at[p, 0], next_y),
            remote(source.at[below], target.at[spots[1]], edge_send.at[p, 1], edge_recv.at[p, 1], last_y),
        ])
    numbers, rows = [], [[] for h in range(HEADS)]
    for d in range(1, NY):
        peer = {"ctx": z * NY + (y + d) % NY}
        numbers.append(remote(ids_ref, id_row.at[y], id_send.at[d - 1], id_recv.at[d - 1], peer))
        for h in range(HEADS):
            rows[h].append(remote(q_ref.at[:, :, head(h)], q_rows[h].at[own_rows],
                                  row_send.at[d - 1, h], row_recv.at[d - 1, h], peer))
    for copy in rows[0]:
        copy.start()
    for copy in numbers:
        copy.start()
    weight = remote(w_ref, w_other, w_sem.at[0], w_sem.at[1], {"mp": sibling})
    weight.start()

    local[0].wait()

    def turn(h):
        for b in range(QB):
            v_cols[h][z * QB + b] = v_own[b, :, head(h)].T

    turn(0)

    def window_score(h):
        row = lax.broadcasted_iota(jnp.int32, (3 * BLK, 1), 0)
        for qb in range(QB):
            first = jnp.where(me + qb == 0, BLK, 0)
            last = jnp.where(me * QB + qb == count * QB - 1, 2 * BLK, 3 * BLK)
            live = (row >= first) & (row < last)
            keys = [k_edge[2 * h] if qb == 0 else k_cols[h][z * QB + qb - 1]]
            keys.append(k_cols[h][z * QB + qb])
            keys.append(k_edge[2 * h + 1] if qb == QB - 1 else k_cols[h][z * QB + qb + 1])
            s = lax.dot_general(jnp.concatenate(keys, axis=0), q_rows[h][y * QB + qb], NT,
                                preferred_element_type=jnp.float32) * SCALE
            s = jnp.where(live, s, LOW)
            top = jnp.max(s, axis=0, keepdims=True)
            p = jnp.exp(s - top).astype(jnp.bfloat16)
            w_stat[qb, pl.ds(h, 1), :] = top
            w_stat[qb, pl.ds(HEADS + h, 1), :] = jnp.sum(p.astype(jnp.float32), axis=0, keepdims=True)
            w_probs[qb, h] = p

    def window_weigh(h):
        for copy in edges[2 * h + 1]:
            copy.wait_recv()
        for qb in range(QB):
            values = [v_edge[2 * h] if qb == 0 else v_cols[h][z * QB + qb - 1]]
            values.append(v_cols[h][z * QB + qb])
            values.append(v_edge[2 * h + 1] if qb == QB - 1 else v_cols[h][z * QB + qb + 1])
            acc[qb, pl.ds(h * HD, HD), :] = jnp.dot(
                jnp.concatenate(values, axis=1), w_probs[qb, h], preferred_element_type=jnp.float32)

    def candidates(t):
        blocks = [glob_ref[j] for j in range(GLOB)]
        blocks += [id_s[lax.div(t, QB), lax.rem(t, QB), j] for j in range(RAND)]
        spots = [lax.div(block, NY * QB) * QB + lax.rem(block, QB) for block in blocks]
        return blocks, spots

    def score(h):
        def one(t, carry):
            blocks, spots = candidates(t)
            bias = [jnp.where(lax.rem(lax.div(block, QB), NY) == y, 0.0, LOW) for block in blocks]
            keys = jnp.concatenate([k_cols[h][spot] for spot in spots], axis=0)
            s = lax.dot_general(keys, q_rows[h][t], NT, preferred_element_type=jnp.float32)
            s = jnp.concatenate([s[j * BLK:(j + 1) * BLK] * SCALE + bias[j] for j in range(CAND)], axis=0)
            top = jnp.max(s, axis=0, keepdims=True)
            p = jnp.exp(s - top).astype(jnp.bfloat16)
            p_stat[h, t, pl.ds(0, 1), :] = top
            p_stat[h, t, pl.ds(1, 1), :] = jnp.sum(p.astype(jnp.float32), axis=0, keepdims=True)
            probs[t, h] = p
            return carry

        return one

    stats = [[] for h in range(HEADS)]
    for d in range(1, NY):
        to = (y + d) % NY
        for h in range(HEADS):
            stats[h].append(remote(p_stat.at[h, pl.ds(to * QB, QB)], got_stat.at[h, d - 1], stat_send.at[h, d - 1],
                                   stat_recv.at[h, d - 1], {"ctx": z * NY + to}))

    def returns(h, i):
        span = pl.ds(h * HD, HD)
        copies = []
        for d in (2, 1, 3):
            to = (y + d) % NY
            copies.append(remote(part.at[to * QB + order[i], span], got.at[d - 1, order[i], span],
                                 part_send.at[h, d - 1, i], part_recv.at[h, d - 1, i], {"ctx": z * NY + to}))
        return copies

    parts = [[returns(h, i) for i in range(QB)] for h in range(HEADS)]

    def weigh(h, i):
        def one(to, carry):
            t = to * QB + order[i]
            spots = candidates(t)[1]
            values = jnp.concatenate([v_cols[h][spot] for spot in spots], axis=1)
            out = jnp.dot(values, probs[t, h], preferred_element_type=jnp.float32)
            out = out / p_stat[h, t, pl.ds(1, 1), :]
            part[t, pl.ds(h * HD, HD), :] = out.astype(jnp.bfloat16)
            return carry

        lax.fori_loop(0, NY, one, 0)
        for copy in parts[h][i]:
            copy.start()

    def merge(h, i):
        for copy in parts[h][i]:
            copy.wait_recv()
        qb = order[i]
        cols = pl.ds(h * HD, HD)
        first, second = pl.ds(0, 1), pl.ds(1, 1)
        tops = [w_stat[qb, pl.ds(h, 1), :], p_stat[h, y * QB + qb, first, :]]
        tops += [got_stat[h, s, qb, first, :] for s in range(NY - 1)]
        sums = [w_stat[qb, pl.ds(HEADS + h, 1), :], p_stat[h, y * QB + qb, second, :]]
        sums += [got_stat[h, s, qb, second, :] for s in range(NY - 1)]
        best = tops[0]
        for top in tops[1:]:
            best = jnp.maximum(best, top)
        scales = [jnp.exp(top - best) for top in tops]
        weights = [scale * total_of for scale, total_of in zip(scales, sums)]
        low = weights[0] + weights[1] + weights[2] + weights[3] + weights[4]
        value = acc[qb, cols, :] * (scales[0] / low)
        value += part[y * QB + qb, cols, :].astype(jnp.float32) * (weights[1] / low)
        for s in range(NY - 1):
            value += got[s, qb, cols, :].astype(jnp.float32) * (weights[s + 2] / low)
        if h == LATE:
            att_late[i] = value.T.astype(jnp.bfloat16)
        else:
            att[i, :, cols] = value.T.astype(jnp.bfloat16)

    mine = pl.ds(pl.multiple_of(core * HALF, HALF), HALF)
    theirs = pl.ds(pl.multiple_of((1 - core) * HALF, HALF), HALF)
    swaps = [remote(att.at[i, theirs], att_other.at[i], att_send.at[i], att_recv.at[i], {"mp": sibling})
             for i in range(QB)]

    def project(group):
        def one(n, carry):
            cols = pl.ds(pl.multiple_of(n * TILE, TILE), TILE)
            own = jnp.concatenate([att[i, mine, :] for i in group], axis=0)
            other = jnp.concatenate([att_other[i] for i in group], axis=0)
            value = jnp.dot(own, w_own[main, cols], preferred_element_type=jnp.float32)
            value += jnp.dot(other, w_other[main, cols], preferred_element_type=jnp.float32)
            for m, i in enumerate(group):
                total[i, :, cols] = value[m * HALF:(m + 1) * HALF]
            return carry

        for i in group:
            swaps[i].wait_recv()
        lax.fori_loop(0, TILES, one, 0)

    far = [[], []]
    for way, peer in enumerate(({"mp": right}, {"mp": left})):
        from_d, to_d = (2, 0)[way], (2, 0)[way]
        for c in range(CUTS):
            rows_of = pl.ds(pl.multiple_of(core * HD + c * CUT, CUT), CUT)
            far[way].append(remote(w_ref.at[pl.ds(MAIN + c * CUT, CUT)], w_far.at[to_d, rows_of],
                                   far_send.at[way, c], far_recv.at[way, c], peer))
        for n in range(CUTS // 2):
            c = n + way * (CUTS // 2)
            rows_of = pl.ds(pl.multiple_of(core * HD + c * CUT, CUT), CUT)
            far[way].append(remote(w_far.at[from_d, rows_of], w_far.at[1, rows_of],
                                   far_send.at[way, CUTS + n], far_recv.at[way, CUTS + n], peer))
    own_half = pl.ds(pl.multiple_of(core * HD, HD), HD)
    passed = [remote(w_far.at[d, own_half], w_far.at[d, own_half], pass_send.at[d], pass_recv.at[d], {"mp": sibling})
              for d in range(NX - 1)]

    lates = []
    for i, qb in enumerate(order):
        lates.append([])
        for c in range(2):
            if i < QB - 1:
                lates[i].append(remote(att_late.at[i, pl.ds(c * HALF, HALF)], come_late.at[mp],
                                       late_send.at[i, c], late_recv.at[i, core], {"mp": qb * 2 + c}))
    lates[QB - 1].append(remote(att_late.at[QB - 1, theirs], come_late.at[mp],
                                late_send.at[QB - 1, 0], late_recv.at[QB - 1, core], {"mp": sibling}))

    sends = [remote(sent.at[0, :, pl.ds(s * MIDDLE, MIDDLE)], relay.at[s], x_send.at[s], x_recv.at[s], {"mp": peer})
             for s, peer in enumerate((right, left))]
    for n in range(2):
        for i, peer in ((1, right), (2, left)):
            side = pl.ds(((i + n) % 2) * MIDDLE, MIDDLE)
            sends.append(remote(sent.at[i, :, side], final.at[i - 1, :, side],
                                x_send.at[1 + 2 * n + i], x_recv.at[1 + 2 * n + i], {"mp": peer}))

    def send_first():
        sent[0] = total[0].astype(jnp.bfloat16)
        sends[0].start()
        sends[1].start()

    def send_direct():
        for i in (1, 2):
            there = pl.ds((i % 2) * MIDDLE, MIDDLE)
            sent[i, :, there] = total[i, :, there].astype(jnp.bfloat16)
            sends[1 + i].start()

    def send_relayed(i):
        sends[i - 1].wait_recv()
        here = pl.ds((i - 1) * MIDDLE, MIDDLE)
        sent[i, :, here] = (total[i, :, here] + relay[i - 1].astype(jnp.float32)).astype(jnp.bfloat16)
        sends[3 + i].start()

    def weights_come():
        weight.wait()
        local[2].wait()

    work = {}

    def at(r, *calls):
        work.setdefault(r, []).extend(calls)

    def edges_go(p):
        if p % 2 == 0:
            k_local[p // 2].wait()
        for copy in edges[p]:
            copy.start()

    def rows_come(h):
        q_local[h].wait()
        for copy in rows[h] + edges[2 * h]:
            copy.wait_recv()
        if h == 0:
            local[1].wait()
            for copy in numbers:
                copy.wait_recv()
            to_scalar = pltpu.make_async_copy(id_row, id_s, local_sem.at[3])
            to_scalar.start()
            to_scalar.wait()

    def stats_go(h):
        for copy in stats[h]:
            copy.start()

    def stats_come(h):
        for copy in stats[h]:
            copy.wait_recv()

    def merge_swap(i):
        merge(LATE - 1, i)
        swaps[i].start()

    def far_go(n):
        for way in range(2):
            if n >= CUTS:
                far[way][n - CUTS + way * (CUTS // 2)].wait_recv()
            far[way][n].start()

    def pass_near():
        for way, d in ((0, 2), (1, 0)):
            for n in range(CUTS // 2):
                far[way][n + (1 - way) * (CUTS // 2)].wait_recv()
            passed[d].start()

    def pass_far():
        for way in range(2):
            for n in range(CUTS, CUTS + CUTS // 2):
                far[way][n].wait_recv()
        passed[1].start()

    for h, r in ((1, 2), (2, 14), (3, 26)):
        for d in range(NY - 1):
            at(r + d, rows[h][d].start)
    for p in range(PHASES):
        at(SPOT[p, 0, 1], lambda p=p: edges_go(p))
    for n, r in enumerate((1, 5, 9, 13, 18, 22)):
        at(r, lambda n=n: far_go(n))
    at(25, pass_near)
    at(31, pass_far)
    for h in range(LATE):
        k, v = DONE[2 * h], DONE[2 * h + 1]
        at(k, lambda h=h: rows_come(h), lambda h=h: window_score(h))
        for n in range(4):
            at(k + 1 + n, lambda h=h, n=n: lax.fori_loop(4 * n, 4 * n + 4, score(h), 0))
        at(k + 5, lambda h=h: stats_go(h))
        for i in range(QB):
            at(v + i // (2 if h == LATE - 1 else 1), lambda h=h, i=i: weigh(h, i))
        at(v + (2 if h == LATE - 1 else QB), lambda h=h: window_weigh(h))
    for h in range(LATE - 1):
        at(DONE[2 * h + 2] + 5, lambda h=h: stats_come(h), lambda h=h: merge(h, 0), lambda h=h: merge(h, 1))
        at(DONE[2 * h + 2] + 6, lambda h=h: merge(h, 2), lambda h=h: merge(h, 3))
    for h in range(1, HEADS):
        at(2 * h, lambda h=h: turn(h))
    v, k = DONE[2 * LATE - 1], DONE[2 * LATE]
    at(v + 3, lambda: stats_come(LATE - 1), lambda: merge_swap(0))
    at(v + 4, weights_come, lambda: project((0,)), send_first)
    at(v + 5, lambda: merge_swap(1), lambda: merge_swap(2), lambda: merge_swap(3))
    at(v + 6, lambda: project((1, 2, 3)), send_direct)
    at(k, lambda: rows_come(LATE), lambda: window_score(LATE), lambda: lax.fori_loop(0, 5, score(LATE), 0))
    at(k + 1, lambda: lax.fori_loop(5, 10, score(LATE), 0))
    at(k + 2, lambda: lax.fori_loop(10, 16, score(LATE), 0), lambda: stats_go(LATE))
    assert max(work) < RING

    for r in range(RING):
        for way in range(2):
            rings[way][r].wait_recv()
            for n in follow.get(r, ()):
                rings[way][n].start()
        for call in work.get(r, ()):
            call()

    for i in range(QB):
        weigh(LATE, i)
    send_relayed(1)
    send_relayed(2)
    window_weigh(LATE)
    stats_come(LATE)
    for i in range(QB):
        merge(LATE, i)
        for copy in lates[i]:
            copy.start()
    come_late[mp] = att_late[QB - 1, mine, :]
    for copy in passed:
        copy.wait_recv()
    for i in range(QB - 1):
        for c in range(2):
            remote(att_late.at[i, pl.ds(0, HALF)], come_late.at[mp], late_send.at[i, c], late_recv.at[i, c],
                   {"mp": sibling}).wait_recv()
    remote(att_late.at[QB - 1, theirs], come_late.at[mp], late_send.at[QB - 1, 0], late_recv.at[QB - 1, 1 - core],
           {"mp": sibling}).wait_recv()
    for copy in sends[2:]:
        copy.wait_recv()

    def finish(n, carry):
        cols = pl.ds(pl.multiple_of(n * TILE, TILE), TILE)
        value = total[QB - 1, :, cols] + jnp.dot(come_late[mp], w_own[late, cols], preferred_element_type=jnp.float32)
        value += jnp.dot(come_late[sibling], w_other[late, cols], preferred_element_type=jnp.float32)
        for d in range(1, NX):
            chip = ((x + d) % NX) * 2
            pair = jnp.concatenate([come_late[chip], come_late[chip + 1]], axis=1)
            value += jnp.dot(pair, w_far[d - 1, :, cols], preferred_element_type=jnp.float32)
        value += final[0, :, cols].astype(jnp.float32) + final[1, :, cols].astype(jnp.float32)
        out_ref[:, cols] = value.astype(jnp.bfloat16)
        return carry

    lax.fori_loop(0, TILES, finish, 0)

    groups = edges + rings + far + lates + stats + rows + [numbers, swaps, sends, passed]
    groups += [c for h in range(HEADS) for c in parts[h]]
    for copies in groups:
        for copy in copies:
            copy.wait_send()


def shards(query_rows, key_rows, value_rows, out_weight, random_ids, global_ids):
    bf, f32 = jnp.bfloat16, jnp.float32
    dma = pltpu.SemaphoreType.DMA
    vmem = pltpu.VMEM
    ids = jnp.pad(random_ids, ((0, 8 - QB), (0, 128 - RAND)))
    anywhere = pl.BlockSpec(memory_space=pl.ANY)
    blocks = (QB, BLK, FEATS)
    return pl.pallas_call(
        kernel,
        name="attend_and_project",
        out_shape=jax.ShapeDtypeStruct((HALF, WIDTH), bf),
        in_specs=[anywhere] * 5 + [pl.BlockSpec(memory_space=pltpu.SMEM)],
        out_specs=pl.BlockSpec(memory_space=pltpu.VMEM),
        scratch_shapes=[
            *[vmem((NZ * QB, BLK, HD), bf)] * HEADS,
            *[vmem((NZ * QB, HD, BLK), bf)] * HEADS,
            *[vmem((NY * QB, BLK, HD), bf)] * HEADS,
            vmem((NY, 8, 128), jnp.int32),
            pltpu.SMEM((NY, 8, 128), jnp.int32),
            vmem((2 * HEADS, BLK, HD), bf),
            vmem((2 * HEADS, HD, BLK), bf),
            vmem(blocks, bf),
            vmem((QB, FEATS, BLK), f32),
            vmem((QB, 2 * HEADS, BLK), f32),
            vmem((QB, HEADS, 3 * BLK, BLK), bf),
            vmem((NY * QB, HEADS, CAND * BLK, BLK), bf),
            vmem((NY * QB, FEATS, BLK), bf),
            vmem((HEADS, NY * QB, 8, BLK), f32),
            vmem((NY - 1, QB, FEATS, BLK), bf),
            vmem((HEADS, NY - 1, QB, 8, BLK), f32),
            vmem((FEATS, WIDTH), bf),
            vmem((FEATS, WIDTH), bf),
            vmem((NX - 1, 2 * HD, WIDTH), bf),
            vmem((QB, BLK, MAIN), bf),
            vmem((QB, HALF, MAIN), bf),
            vmem((QB, BLK, HD), bf),
            vmem((2 * NX, HALF, HD), bf),
            vmem((3, HALF, WIDTH), bf),
            vmem((2, HALF, WIDTH // 2), bf),
            vmem((2, HALF, WIDTH), bf),
            vmem((QB, HALF, WIDTH), f32),
            dma((2, RING)), dma((2, RING)), dma((NY - 1, HEADS)), dma((NY - 1, HEADS)), dma((NY - 1,)), dma((NY - 1,)),
            dma((PHASES, 2)), dma((PHASES, 2)), dma((2,)), dma((12,)),
            dma((HEADS, NY - 1, QB)), dma((HEADS, NY - 1, QB)), dma((HEADS, NY - 1)), dma((HEADS, NY - 1)),
            dma((QB,)), dma((QB,)), dma((6,)), dma((6,)),
            dma((2, 6)), dma((2, 6)), dma((NX - 1,)), dma((NX - 1,)), dma((QB, 2)), dma((QB, 2)),
        ],
        compiler_params=pltpu.CompilerParams(
            collective_id=0, has_side_effects=True, vmem_limit_bytes=60 * MIB
        ),
        cost_estimate=pl.CostEstimate(flops=4 * 10**9, bytes_accessed=24 * MIB, transcendentals=0),
    )(
        query_rows.reshape(blocks), key_rows.reshape(blocks), value_rows.reshape(blocks),
        out_weight, ids, global_ids,
    )


def solution(mesh):
    return jax.shard_map(
        shards,
        mesh=mesh,
        in_specs=(
            P("ctx", "mp"),
            P("ctx", "mp"),
            P("ctx", "mp"),
            P("mp", None),
            P("ctx", None),
            P(),
        ),
        out_specs=P(("ctx", "mp"), None),
        check_vma=False,
    )
```

time: 129 us -> 121 us (0.938)
  Pallas kernels: 125 us -> 117 us
    pallas_call x1, Pallas kernels: 125 us -> 117 us  [shards(): pl.pallas_call(kernel, name='attend_and_project', out_shape=jax.ShapeDtyp...]
where the time goes in v5:
time: 121 us; the launch traced here: 120 us
  Pallas kernels  117 us (97%)
  local copies, waits for them, and re-layouts  3.15 us (3%)
    pallas_call x1, Pallas kernels, shards(): pl.pallas_call(kernel, name='attend_and_project', out_shape=jax.ShapeDtyp...  117 us

profile of v5, /device:TPU:1, one launch (start us, length us, event | category | flops | bytes accessed | tf_op | source)
XLA Modules:
  0.0 120.4 jit_solution(7376698638260567095)
XLA Ops:
  0.0 1.3 %pad.4.ids_ref = s32[8,128]{1,0:T(8,128)} pad(s32[4,3]{1,0:T(4,128)} %param.10, s32[]{:T(128)} %constant.0.clone.1), padding=0_4x0_125 | pad | bytes 4148 | tf_op jit(solution)/shard_map/jit(_pad)/pad | solution.py:490
  1.3 117.2 %attend_and_project.1 = bf16[64,4096]{1,0:T(8,128)(2,1)} custom-call(bf16[4,128,512]{2,1,0:T(8,128)(2,1)} %bitcast.3, bf16[4,128,512]{2,1,0:T(8,128)(2,1)} %bitcast.4, bf16[4,128,512]{2,1,0:T(8,128)(2,1)} %bitcast.5, bf16[512,4096]{1,0:T(8,128)(2,1)} %w_ref.1, s32[8,128]{1,0:T(8,128)} %pad.4.ids_ref, s32[2]{0:T(128)} %glob_ref.1), custom_call_target="tpu_custom_call" | custom-call | flops 4000000000 | bytes 25165824 | tf_op jit(solution)/shard_map/attend_and_project/pallas_call | solution.py:493
  118.5 1.9 %copy.8 = bf16[64,4096]{1,0:T(8,128)(2,1)} copy(bf16[64,4096]{1,0:T(8,128)(2,1)} %attend_and_project.1) | data formatting | bytes 1048576

commit v6 on v5

--- a/solution.py
+++ b/solution.py
@@ -242,7 +242,7 @@
             part[t, pl.ds(h * HD, HD), :] = out.astype(jnp.bfloat16)
             return carry
 
-        lax.fori_loop(0, NY, one, 0)
+        lax.fori_loop(0, NY, one, 0, unroll=True)
         for copy in parts[h][i]:
             copy.start()
 
@@ -289,7 +289,7 @@
 
         for i in group:
             swaps[i].wait_recv()
-        lax.fori_loop(0, TILES, one, 0)
+        lax.fori_loop(0, TILES, one, 0, unroll=True)
 
     far = [[], []]
     for way, peer in enumerate(({"mp": right}, {"mp": left})):
@@ -412,24 +412,24 @@
         k, v = DONE[2 * h], DONE[2 * h + 1]
         at(k, lambda h=h: rows_come(h), lambda h=h: window_score(h))
         for n in range(4):
-            at(k + 1 + n, lambda h=h, n=n: lax.fori_loop(4 * n, 4 * n + 4, score(h), 0))
+            at(k + 1 + n, lambda h=h, n=n: lax.fori_loop(4 * n, 4 * n + 4, score(h), 0, unroll=True))
         at(k + 5, lambda h=h: stats_go(h))
         for i in range(QB):
             at(v + i // (2 if h == LATE - 1 else 1), lambda h=h, i=i: weigh(h, i))
-        at(v + (2 if h == LATE - 1 else QB), lambda h=h: window_weigh(h))
+        at(v + (1 if h == LATE - 1 else QB), lambda h=h: window_weigh(h))
     for h in range(LATE - 1):
         at(DONE[2 * h + 2] + 5, lambda h=h: stats_come(h), lambda h=h: merge(h, 0), lambda h=h: merge(h, 1))
         at(DONE[2 * h + 2] + 6, lambda h=h: merge(h, 2), lambda h=h: merge(h, 3))
     for h in range(1, HEADS):
         at(2 * h, lambda h=h: turn(h))
     v, k = DONE[2 * LATE - 1], DONE[2 * LATE]
-    at(v + 3, lambda: stats_come(LATE - 1), lambda: merge_swap(0))
-    at(v + 4, weights_come, lambda: project((0,)), send_first)
-    at(v + 5, lambda: merge_swap(1), lambda: merge_swap(2), lambda: merge_swap(3))
-    at(v + 6, lambda: project((1, 2, 3)), send_direct)
-    at(k, lambda: rows_come(LATE), lambda: window_score(LATE), lambda: lax.fori_loop(0, 5, score(LATE), 0))
-    at(k + 1, lambda: lax.fori_loop(5, 10, score(LATE), 0))
-    at(k + 2, lambda: lax.fori_loop(10, 16, score(LATE), 0), lambda: stats_go(LATE))
+    at(v + 2, lambda: stats_come(LATE - 1), lambda: merge_swap(0))
+    at(v + 3, weights_come, lambda: project((0,)), send_first)
+    at(v + 4, lambda: merge_swap(1), lambda: merge_swap(2), lambda: merge_swap(3))
+    at(v + 5, lambda: project((1, 2, 3)), send_direct)
+    at(k, lambda: rows_come(LATE), lambda: window_score(LATE), lambda: lax.fori_loop(0, 5, score(LATE), 0, unroll=True))
+    at(k + 1, lambda: lax.fori_loop(5, 10, score(LATE), 0, unroll=True))
+    at(k + 2, lambda: lax.fori_loop(10, 16, score(LATE), 0, unroll=True), lambda: stats_go(LATE))
     assert max(work) < RING
 
     for r in range(RING):
@@ -459,8 +459,6 @@
                    {"mp": sibling}).wait_recv()
     remote(att_late.at[QB - 1, theirs], come_late.at[mp], late_send.at[QB - 1, 0], late_recv.at[QB - 1, 1 - core],
            {"mp": sibling}).wait_recv()
-    for copy in sends[2:]:
-        copy.wait_recv()
 
     def finish(n, carry):
         cols = pl.ds(pl.multiple_of(n * TILE, TILE), TILE)
@@ -470,11 +468,20 @@
             chip = ((x + d) % NX) * 2
             pair = jnp.concatenate([come_late[chip], come_late[chip + 1]], axis=1)
             value += jnp.dot(pair, w_far[d - 1, :, cols], preferred_element_type=jnp.float32)
-        value += final[0, :, cols].astype(jnp.float32) + final[1, :, cols].astype(jnp.float32)
-        out_ref[:, cols] = value.astype(jnp.bfloat16)
+        total[QB - 1, :, cols] = value
         return carry
 
-    lax.fori_loop(0, TILES, finish, 0)
+    lax.fori_loop(0, TILES, finish, 0, unroll=True)
+    for copy in sends[2:]:
+        copy.wait_recv()
+
+    def add(n, carry):
+        cols = pl.ds(pl.multiple_of(n * TILE, TILE), TILE)
+        value = final[0, :, cols].astype(jnp.float32) + final[1, :, cols].astype(jnp.float32)
+        out_ref[:, cols] = (total[QB - 1, :, cols] + value).astype(jnp.bfloat16)
+        return carry
+
+    lax.fori_loop(0, TILES, add, 0, unroll=True)
 
     groups = edges + rings + far + lates + stats + rows + [numbers, swaps, sends, passed]
     groups += [c for h in range(HEADS) for c in parts[h]]

time: 121 us -> 116 us (0.959)
  Pallas kernels: 117 us -> 113 us
    pallas_call x1, Pallas kernels: 117 us -> 113 us  [shards(): pl.pallas_call(kernel, name='attend_and_project', out_shape=jax.ShapeDtyp...]
where the time goes in v6:
time: 116 us
  Pallas kernels  113 us (97%)
  local copies, waits for them, and re-layouts  3.15 us (3%)
    pallas_call x1, Pallas kernels, shards(): pl.pallas_call(kernel, name='attend_and_project', out_shape=jax.ShapeDtyp...  113 us

profile of v6, /device:TPU:1, one launch (start us, length us, event | category | flops | bytes accessed | tf_op | source)
XLA Modules:
  0.0 116.1 jit_solution(14327660778671193740)
XLA Ops:
  0.0 1.3 %pad.4.ids_ref = s32[8,128]{1,0:T(8,128)} pad(s32[4,3]{1,0:T(4,128)} %param.10, s32[]{:T(128)} %constant.0.clone.1), padding=0_4x0_125 | pad | bytes 4148 | tf_op jit(solution)/shard_map/jit(_pad)/pad | solution.py:497
  1.3 112.9 %attend_and_project.1 = bf16[64,4096]{1,0:T(8,128)(2,1)} custom-call(bf16[4,128,512]{2,1,0:T(8,128)(2,1)} %bitcast.3, bf16[4,128,512]{2,1,0:T(8,128)(2,1)} %bitcast.4, bf16[4,128,512]{2,1,0:T(8,128)(2,1)} %bitcast.5, bf16[512,4096]{1,0:T(8,128)(2,1)} %w_ref.1, s32[8,128]{1,0:T(8,128)} %pad.4.ids_ref, s32[2]{0:T(128)} %glob_ref.1), custom_call_target="tpu_custom_call" | custom-call | flops 4000000000 | bytes 25165824 | tf_op jit(solution)/shard_map/attend_and_project/pallas_call | solution.py:500
  114.2 1.9 %copy.8 = bf16[64,4096]{1,0:T(8,128)(2,1)} copy(bf16[64,4096]{1,0:T(8,128)(2,1)} %attend_and_project.1) | data formatting | bytes 1048576

commit v7 on v6

--- a/solution.py
+++ b/solution.py
@@ -411,9 +411,10 @@
     for h in range(LATE):
         k, v = DONE[2 * h], DONE[2 * h + 1]
         at(k, lambda h=h: rows_come(h), lambda h=h: window_score(h))
-        for n in range(4):
-            at(k + 1 + n, lambda h=h, n=n: lax.fori_loop(4 * n, 4 * n + 4, score(h), 0, unroll=True))
-        at(k + 5, lambda h=h: stats_go(h))
+        bounds = (0, 4, 8, 12, 16) if h == 0 else (0, 3, 6, 9, 12, 14, 16)
+        for n in range(len(bounds) - 1):
+            at(k + 1 + n, lambda h=h, low=bounds[n], high=bounds[n + 1]: lax.fori_loop(low, high, score(h), 0, unroll=True))
+        at(k + len(bounds) - 1, lambda h=h: stats_go(h))
         for i in range(QB):
             at(v + i // (2 if h == LATE - 1 else 1), lambda h=h, i=i: weigh(h, i))
         at(v + (1 if h == LATE - 1 else QB), lambda h=h: window_weigh(h))

time: 116 us -> 116 us (level)
  no operation moved by 1% of the time
where the time goes in v7:
time: 116 us
  Pallas kernels  113 us (97%)
  local copies, waits for them, and re-layouts  3.15 us (3%)
    pallas_call x1, Pallas kernels, shards(): pl.pallas_call(kernel, name='attend_and_project', out_shape=jax.ShapeDtyp...  113 us

profile of v7, /device:TPU:1, one launch (start us, length us, event | category | flops | bytes accessed | tf_op | source)
XLA Modules:
  0.0 115.9 jit_solution(11267605444332728129)
XLA Ops:
  0.0 1.3 %pad.4.ids_ref = s32[8,128]{1,0:T(8,128)} pad(s32[4,3]{1,0:T(4,128)} %param.10, s32[]{:T(128)} %constant.0.clone.1), padding=0_4x0_125 | pad | bytes 4148 | tf_op jit(solution)/shard_map/jit(_pad)/pad | solution.py:498
  1.3 112.8 %attend_and_project.1 = bf16[64,4096]{1,0:T(8,128)(2,1)} custom-call(bf16[4,128,512]{2,1,0:T(8,128)(2,1)} %bitcast.3, bf16[4,128,512]{2,1,0:T(8,128)(2,1)} %bitcast.4, bf16[4,128,512]{2,1,0:T(8,128)(2,1)} %bitcast.5, bf16[512,4096]{1,0:T(8,128)(2,1)} %w_ref.1, s32[8,128]{1,0:T(8,128)} %pad.4.ids_ref, s32[2]{0:T(128)} %glob_ref.1), custom_call_target="tpu_custom_call" | custom-call | flops 4000000000 | bytes 25165824 | tf_op jit(solution)/shard_map/attend_and_project/pallas_call | solution.py:501
  114.0 1.9 %copy.8 = bf16[64,4096]{1,0:T(8,128)(2,1)} copy(bf16[64,4096]{1,0:T(8,128)(2,1)} %attend_and_project.1) | data formatting | bytes 1048576
